TPU v7x, 128 devices: a whole 4x4x4 slice. The times are simulated.
128 devices in a mesh: mem: 8 (over x_hi, y), tile: 16 (over x_lo, z, core).
Axes of the slice: x: 4 (x_hi: 2, x_lo: 2; x = x_hi * 2 + x_lo), y: 4, z: 4, core: 2. Of those that a mesh axis runs over, the one named last changes fastest.
Arguments:
- background_sample: bfloat16 [128, 227, 16384], P(('mem', 'tile')), may hold values from -6 to 6
- measured_reading: float32 [4, 512], replicated, may hold values from -8 to 8
- measurement_noise_variance: float32 [4, 512], replicated, may hold values from 0.25 to 1
- measurements_in_batch: int32 [4], replicated, may hold values from 256 to 512, as said below
- measurement_patch: int32 [4, 512, 1], replicated, may hold values from 0 to 127; in each aligned block of 512 rows (0 to 511, 512 to 1023, ..., all dimensions but the last counted through in order) at most 16 rows name the same one
- measurement_stack: int32 [4, 512], replicated, may hold values from 0 to 127
- measured_field: int32 [4, 512], replicated, may hold values from 0 to 226
- patch_measurement_roster: int32 [4, 128, 128], P(None, ('mem', 'tile')), may hold values from 0 to 511, as said below
- entry_damping_kind: int32 [4, 128, 128], P(None, ('mem', 'tile')), may hold values from 0 to 8
Outputs:
- analysis: bfloat16 [128, 227, 16384], P(None, None, ('mem', 'tile'))
Inputs may be any that keep to these rules, and one draw needn't show every extreme that they name: A batch's first measurements_in_batch observations are in use; some batch uses all 512. `measurement_patch`: no tile holds more than 16 observations of one batch. `patch_measurement_roster`: the observations in one tile's list of one batch are distinct.
All inputs are finite; a program needn't handle non-finite values.
Results may differ from a plain program's by a relative error of at most 0.0023.
Values may be sent and summed in bfloat16 or wider, within the bound.
No kernel may reach another device: no remote copies, remote signals or barrier semaphores. Data moves between devices by JAX's collectives and lax.ppermute only.
A program may use at most 192 MiB of HBM per device.

v0:
```python
import jax
import jax.numpy as jnp
from jax import lax
from jax.sharding import PartitionSpec as P

OWN_MAX = 16
CLASSES = 8


def analyse(realization_fields, prior_rows, weight, observed, variance):
    realization_number = realization_fields.shape[0]
    inverse_root = 1.0 / jnp.sqrt(jnp.float32(realization_number - 1))
    obs_mean = jnp.mean(prior_rows, axis=1)
    scaled = weight[:, None] * (prior_rows - obs_mean[:, None]) * inverse_root
    innovation = weight * (observed - obs_mean)
    covariance = jnp.dot(scaled, scaled.T, precision=lax.Precision.HIGHEST) + jnp.diag(variance)
    factor = jnp.linalg.cholesky(covariance)
    solved = jax.scipy.linalg.cho_solve((factor, True), scaled)
    solved_d = jax.scipy.linalg.cho_solve((factor, True), innovation[:, None])
    mixing = jnp.dot(scaled.T, solved, precision=lax.Precision.HIGHEST)
    shift_vec = jnp.dot(scaled.T, solved_d, precision=lax.Precision.HIGHEST) * inverse_root
    transform = jnp.eye(realization_number, dtype=jnp.float32) - 0.5 * mixing + shift_vec
    centre = jnp.mean(realization_fields, axis=0)
    spread = realization_fields - centre[None, :]
    return centre[None, :] + jnp.dot(transform.T, spread, precision=lax.Precision.HIGHEST)


def local(
    background_sample,
    measured_reading,
    measurement_noise_variance,
    measurements_in_batch,
    measurement_patch,
    measurement_stack,
    measured_field,
    patch_measurement_roster,
    entry_damping_kind,
):
    realization_number = lax.axis_size(("mem", "tile"))
    myself = lax.axis_index(("mem", "tile"))
    batches = measured_reading.shape[0]
    field_number = background_sample.shape[1]
    stack_extent = background_sample.shape[2] // realization_number
    first_rows = None
    grouped_per_tile = lax.all_to_all(
        background_sample, ("mem", "tile"), split_axis=2, concat_axis=0, tiled=True
    )
    realization_fields = grouped_per_tile.reshape(
        realization_number, field_number * stack_extent
    ).astype(jnp.float32)
    tile_ids = jnp.arange(realization_number, dtype=jnp.int32)
    slot_ids = jnp.arange(OWN_MAX, dtype=jnp.int32)
    for batch_num in range(batches):
        owner = measurement_patch[batch_num, :, 0]
        flat_index = measured_field[batch_num] * stack_extent + measurement_stack[batch_num]
        listed = patch_measurement_roster[batch_num, 0]
        classes = entry_damping_kind[batch_num, 0]
        mine = owner == myself
        matches = (owner[:, None] == tile_ids[None, :]).astype(jnp.int32)
        earlier = jnp.cumsum(matches, axis=0) - matches
        order_in = jnp.sum(earlier * matches, axis=1)
        slot_index = owner * OWN_MAX + order_in
        picked = jnp.logical_and(mine[None, :], order_in[None, :] == slot_ids[:, None])
        picked_index = jnp.sum(jnp.where(picked, flat_index[None, :], 0), axis=1)
        present = jnp.any(picked, axis=1)
        owned = jnp.where(
            present[:, None], jnp.take(realization_fields, picked_index, axis=1).T, jnp.float32(0.0)
        )
        gathered = lax.all_gather(owned, ("mem", "tile"), axis=0, tiled=True)
        prior_rows = jnp.take(gathered, jnp.take(slot_index, listed), axis=0)
        tapered = jnp.where(
            classes > 0, (CLASSES + 1 - classes).astype(jnp.float32) / CLASSES, jnp.float32(0.0)
        )
        weight = tapered * (listed < measurements_in_batch[batch_num]).astype(jnp.float32)
        observed = jnp.take(measured_reading[batch_num], listed)
        variance = jnp.take(measurement_noise_variance[batch_num], listed)
        realization_fields = analyse(realization_fields, prior_rows, weight, observed, variance)
    return realization_fields.reshape(realization_number, field_number, stack_extent).astype(
        jnp.bfloat16
    )


def solution(mesh):
    in_specs = (
        P(("mem", "tile"), None, None),
        P(),
        P(),
        P(),
        P(),
        P(),
        P(),
        P(None, ("mem", "tile"), None),
        P(None, ("mem", "tile"), None),
    )
    out_specs = P(None, None, ("mem", "tile"))
    return jax.shard_map(local, mesh=mesh, in_specs=in_specs, out_specs=out_specs, check_vma=False)
```

profile of v0, /device:TPU:1, one launch (start us, length us, event | category | flops | bytes accessed | tf_op | source)
XLA Modules:
  0.0 1437.5 jit_solution(9810628635615999355)
XLA Ops:
  6.5 34.3 %copy.166 = bf16[1,227,16384]{1,0,2:T(2,128)(2,1)} copy(bf16[1,227,16384]{2,1,0:T(8,128)(2,1)} %param.22) | data formatting | bytes 14876672 | tf_op args[0]
  41.4 92.8 %reduce.7 = bf16[16384,227]{1,0:T(8,128)(2,1)} reduce(bf16[16384,1,227]{2,1,0:T(2,128)(2,1)} %bitcast.307, bf16[]{:T(256)} %broadcast.630), dimensions={1}, to_apply=%bitcast.265.reduce_sub_computation | reduce | bytes 14876674
  134.2 24.2 %reshape.577 = bf16[128,2,14528]{2,1,0:T(2,128)(2,1)} reshape(bf16[16384,227]{1,0:T(8,128)(2,1)} %reduce.7) | data formatting | bytes 14876672
  158.4 11.9 all-to-all-start
  177.0 83.9 %all-to-all-done = bf16[128,2,14528]{2,1,0:T(2,128)(2,1)} async-done(((bf16[128,2,14528]{2,1,0:T(2,128)(2,1)}), bf16[128,2,14528]{2,1,0:T(2,128)(2,1)}, u32[]{:S(2)}, u32[]{:S(2)}) %all-to-all-start) | async-done | bytes 7438368 | tf_op jit(solution)/shard_map/all_to_all | solution.py:45
  260.9 44.4 %reshape.578 = bf16[16384,1,227]{2,1,0:T(2,128)(2,1)} reshape(bf16[128,2,14528]{2,1,0:T(2,128)(2,1)} %all-to-all-done) | data formatting | bytes 14876672
  305.3 33.2 %copy.167 = bf16[1,227,16384]{2,1,0:T(8,128)(2,1)} copy(bf16[1,227,16384]{1,0,2:T(2,128)(2,1)} %bitcast.308) | data formatting | bytes 14876672 | tf_op jit(solution)/shard_map/all_to_all | solution.py:45
  338.5 10.3 convert_element_type.122
  348.8 13.5 copy.203
  362.4 14.5 %slice_reduce_fusion = (f32[227,128]{1,0:T(8,128)S(1)}, f32[128,1,227,128]{3,0,1,2:T(8,128)}) fusion(f32[232,128,128]{2,1,0:T(8,128)} %bitcast.312), kind=kLoop, calls=%fused_computation.30 | loop fusion | flops 3690112 | bytes 29869568 | tf_op jit(solution)/shard_map/reduce_sum | solution.py:23
  376.8 15.2 %copy.170 = f32[128,1,227,128]{0,3,2,1:T(8,128)} copy(f32[128,1,227,128]{3,0,1,2:T(8,128)} %get-tuple-element.21) | data formatting | bytes 29753344 | tf_op jit(solution)/shard_map/convert_element_type | solution.py:50
  404.2 15.2 %copy.174 = f32[128,29056]{1,0:T(8,128)} copy(f32[128,29056]{0,1:T(8,128)} %bitcast.310) | data formatting | bytes 29753344 | tf_op jit(solution)/shard_map/convert_element_type | solution.py:50
  419.5 169.1 %all-gather.5.cloned.1.call-done = f32[2048,128]{1,0:T(8,128)} async-done(((f32[16,128]{1,0:T(8,128)}), f32[2048,128]{1,0:T(8,128)}) %all-gather.5.cloned.1.call-update) | async-done | bytes 1048592 | tf_op jit(solution)/shard_map/all_gather | solution.py:69
  591.0 11.7 cholesky.74
  604.1 9.8 custom-call.18
  615.5 20.2 %fusion.113 = (f32[29056]{0:T(1024)S(1)}, f32[128,29056]{1,0:T(8,128)}) fusion(f32[128,128]{0,1:T(8,128)S(1)} %fusion.16, f32[128,29056]{1,0:T(8,128)} %copy.174, f32[29056]{0:T(1024)S(1)} %multiply_bitcast_fusion), kind=kOutput, calls=%fused_computation.286 | convolution fusion | flops 5723770368 | bytes 30051328 | tf_op jit(solution)/shard_map/dot_general | solution.py:25
  635.7 15.2 %copy.177 = f32[128,29056]{0,1:T(8,128)} copy(f32[128,29056]{1,0:T(8,128)} %get-tuple-element.51) | data formatting | bytes 29753344 | tf_op jit(solution)/shard_map/add | solution.py:25
  661.8 184.9 %all-gather.7.cloned.1.call-done = f32[2048,128]{1,0:T(8,128)} async-done(((f32[16,128]{1,0:T(8,128)}), f32[2048,128]{1,0:T(8,128)}) %all-gather.7.cloned.1.call-update) | async-done | bytes 1048592 | tf_op jit(solution)/shard_map/all_gather | solution.py:69
  849.2 11.7 cholesky.85
  862.3 9.8 custom-call.20
  873.7 20.5 %fusion.114 = (f32[29056]{0:T(1024)S(1)}, f32[128,29056]{1,0:T(8,128)}) fusion(f32[128,128]{0,1:T(8,128)S(1)} %fusion.14, f32[128,29056]{1,0:T(8,128)} %get-tuple-element.51, f32[29056]{0:T(1024)S(1)} %broadcast_multiply_fusion.2), kind=kOutput, calls=%fused_computation.287 | convolution fusion | flops 5723770368 | bytes 30051328 | tf_op jit(solution)/shard_map/dot_general | solution.py:25
  894.2 15.2 %copy.183 = f32[128,29056]{0,1:T(8,128)} copy(f32[128,29056]{1,0:T(8,128)} %get-tuple-element.53) | data formatting | bytes 29753344 | tf_op jit(solution)/shard_map/add | solution.py:25
  919.3 185.9 %all-gather.9.cloned.1.call-done = f32[2048,128]{1,0:T(8,128)} async-done(((f32[16,128]{1,0:T(8,128)}), f32[2048,128]{1,0:T(8,128)}) %all-gather.9.cloned.1.call-update) | async-done | bytes 1048592 | tf_op jit(solution)/shard_map/all_gather | solution.py:69
  1107.8 11.7 cholesky.96
  1120.8 9.8 custom-call.22
  1132.2 20.2 %fusion.115 = (f32[29056]{0:T(1024)S(1)}, f32[128,29056]{1,0:T(8,128)}) fusion(f32[128,128]{0,1:T(8,128)S(1)} %fusion.12, f32[128,29056]{1,0:T(8,128)} %get-tuple-element.53, f32[29056]{0:T(1024)S(1)} %broadcast_multiply_fusion.1), kind=kOutput, calls=%fused_computation.288 | convolution fusion | flops 5723770368 | bytes 30051328 | tf_op jit(solution)/shard_map/dot_general | solution.py:25
  1152.4 15.2 %copy.189 = f32[128,29056]{0,1:T(8,128)} copy(f32[128,29056]{1,0:T(8,128)} %get-tuple-element.55) | data formatting | bytes 29753344 | tf_op jit(solution)/shard_map/add | solution.py:25
  1178.3 185.1 %all-gather.11.cloned.1.call-done = f32[2048,128]{1,0:T(8,128)} async-done(((f32[16,128]{1,0:T(8,128)}), f32[2048,128]{1,0:T(8,128)}) %all-gather.11.cloned.1.call-update) | async-done | bytes 1048592 | tf_op jit(solution)/shard_map/all_gather | solution.py:69
  1366.0 11.7 cholesky.107
  1390.5 19.2 %fusion = bf16[128,29056]{1,0:T(8,128)(2,1)} fusion(f32[128,128]{0,1:T(8,128)S(1)} %fusion.10, f32[128,29056]{1,0:T(8,128)} %get-tuple-element.55, f32[29056]{0:T(1024)S(1)} %broadcast_multiply_fusion), kind=kOutput, calls=%fused_computation.24 | convolution fusion | flops 5723799552 | bytes 22496768 | tf_op jit(solution)/shard_map/dot_general | solution.py:25
  1409.7 10.4 copy.193
  1420.1 10.4 copy.194
  (194 shorter events, 81.6 us)
Async XLA Ops:
  134.2 36.7 %copy-start.3 = (s32[4,512,1]{1,2,0:T(1,128)S(1)}, s32[4,512,1]{1,2,0:T(1,128)}, u32[]{:S(2)}) copy-start(s32[4,512,1]{1,2,0:T(1,128)} %param.26) | copy-start | bytes 24580
  134.2 38.0 %copy-start.2 = (s32[4,1,128]{2,1,0:T(1,128)S(1)}, s32[4,1,128]{2,1,0:T(1,128)}, u32[]{:S(2)}) copy-start(s32[4,1,128]{2,1,0:T(1,128)} %param.29) | copy-start | bytes 6148
  134.2 41.1 %copy-start = (s32[4,512]{1,0:T(4,128)S(1)}, s32[4,512]{1,0:T(4,128)}, u32[]{:S(2)}) copy-start(s32[4,512]{1,0:T(4,128)} %param.27) | copy-start | bytes 24580
  134.2 41.1 %copy-start.1 = (s32[4,512]{1,0:T(4,128)S(1)}, s32[4,512]{1,0:T(4,128)}, u32[]{:S(2)}) copy-start(s32[4,512]{1,0:T(4,128)} %param.28) | copy-start | bytes 24580
  134.2 41.5 %copy-start.6 = (s32[4]{0:T(128)S(1)}, s32[4]{0:T(128)}, u32[]{:S(2)}) copy-start(s32[4]{0:T(128)} %param.25) | copy-start | bytes 52
  134.2 42.8 %copy-start.4 = (f32[4,512]{1,0:T(4,128)S(1)}, f32[4,512]{1,0:T(4,128)}, u32[]{:S(2)}) copy-start(f32[4,512]{1,0:T(4,128)} %param.24) | copy-start | bytes 24580
  134.2 42.8 %copy-start.5 = (f32[4,512]{1,0:T(4,128)S(1)}, f32[4,512]{1,0:T(4,128)}, u32[]{:S(2)}) copy-start(f32[4,512]{1,0:T(4,128)} %param.23) | copy-start | bytes 24580
  158.4 102.5 %all-to-all-start = ((bf16[128,2,14528]{2,1,0:T(2,128)(2,1)}), bf16[128,2,14528]{2,1,0:T(2,128)(2,1)}, u32[]{:S(2)}, u32[]{:S(2)}) async-start(bf16[128,2,14528]{2,1,0:T(2,128)(2,1)} %reshape.577), calls=%async_computation | async-start | bytes 14942208 | tf_op jit(solution)/shard_map/all_to_all | solution.py:45
  170.3 418.2 %all-gather.5.cloned.1.call-start = ((), (), s32[]{:S(2)}) async-start(), calls=%async_computation.1 | async-start | bytes 1056768 | tf_op jit(solution)/shard_map/all_gather | solution.py:69
  376.8 24.9 %copy-start.7 = (s32[4,1,128]{2,1,0:T(1,128)S(1)}, s32[4,1,128]{2,1,0:T(1,128)}, u32[]{:S(2)}) copy-start(s32[4,1,128]{2,1,0:T(1,128)} %param.30) | copy-start | bytes 6148
  398.6 448.1 %all-gather.7.cloned.1.call-start = ((), (), s32[]{:S(2)}) async-start(), calls=%async_computation.2 | async-start | bytes 1056768 | tf_op jit(solution)/shard_map/all_gather | solution.py:69
  657.4 447.8 %all-gather.9.cloned.1.call-start = ((), (), s32[]{:S(2)}) async-start(), calls=%async_computation.3 | async-start | bytes 1056768 | tf_op jit(solution)/shard_map/all_gather | solution.py:69
  916.0 447.5 %all-gather.11.cloned.1.call-start = ((), (), s32[]{:S(2)}) async-start(), calls=%async_computation.4 | async-start | bytes 1056768 | tf_op jit(solution)/shard_map/all_gather | solution.py:69
Sparse Core Ops, SparseCore 0:
  398.7 189.7 all-gather.4
  657.5 189.1 all-gather.6
  916.1 189.1 all-gather.8
  1174.3 189.1 all-gather.10
where the time goes:
time: 1450 us; the launch traced here: 1440 us
  waiting for transfers between devices  809 us (56%)
  local copies, waits for them, and re-layouts  295 us (20%)
  other arithmetic  218 us (15%)
  matrix products  87.9 us (6%)
  between operations  14.5 us (1%)
    all_gather x4, waiting for transfers between devices, local(): gathered = lax.all_gather(owned, ('mem', 'tile'), axis=0, tiled=True)  725 us
    unnamed x25, local copies, waits for them, and re-layouts  117 us
    unnamed x1, other arithmetic  92.8 us
    all_to_all x1, waiting for transfers between devices, local(): lax.all_to_all(background_sample, ('mem', 'tile'), split_axis=2, concat_a...  83.9 us
    dot_general x4, matrix products, analyse(): jnp.dot(transform.T, spread, precision=lax.Precision.HIGHEST)  80.1 us
    another operation x12, other arithmetic, analyse(): factor = jnp.linalg.cholesky(covariance)  49.6 us
    add x3, local copies, waits for them, and re-layouts, analyse(): centre[None, :]  45.7 us
    another operation x8, other arithmetic, analyse(): solved = jax.scipy.linalg.cho_solve((factor, True), scaled)  41.9 us
  transfers between devices with their start and end apart: 5, of which 5 were waited for; matrix products, arithmetic and copies ran while one was open for 3% of the time, Pallas kernels for 0%

commit v1 on v0

v1 whole, which is shorter than its diff:
```python
import functools
import jax
import jax.numpy as jnp
from jax import lax
from jax.experimental import pallas as pl
from jax.experimental.pallas import tpu as pltpu
from jax.sharding import PartitionSpec as P

OWN_MAX = 16
CLASSES = 8
AXES = ("mem", "tile")
BATCHES = 4
OBS = 512
TILES = 128
MEMBERS = 128
LANES = 128
FIELDS = 227
SLOTS = BATCHES * OWN_MAX
GROUP = 8
VMEM_LIMIT = 48 * 1024 * 1024
HIGHEST = lax.Precision.HIGHEST
F32 = jnp.float32
BF16 = jnp.bfloat16
INVERSE_ROOT = 1.0 / (MEMBERS - 1) ** 0.5


def iota(shape, dim):
    return lax.broadcasted_iota(jnp.int32, shape, dim)


def dot(a, b, precision=None):
    return jnp.dot(a, b, precision=precision, preferred_element_type=F32)


def dot_nt(a, b):
    return lax.dot_general(a, b, (((1,), (1,)), ((), ())), preferred_element_type=F32)


def owner_order(owner_row):
    hot = iota((TILES, OBS), 0) == owner_row
    hot_f = jnp.where(hot, 1.0, 0.0)
    before = jnp.where(iota((OBS, OBS), 0) < iota((OBS, OBS), 1), 1.0, 0.0).astype(BF16)
    counts = dot(hot_f.astype(BF16), before)
    order = jnp.sum(hot_f * counts, axis=0, keepdims=True)
    return hot_f, order


def sort_out_kernel(x_ref, owner_ref, field_ref, stack_ref, blocks_ref, message_ref, table_ref, values_ref):
    step = pl.program_id(0)

    @pl.when(step == 0)
    def _():
        for b in range(BATCHES):
            hot, order = owner_order(owner_ref[b : b + 1, :])
            slot_hot = iota((OWN_MAX, OBS), 0).astype(F32) == order
            fields = jnp.where(slot_hot, field_ref[b : b + 1, :].astype(F32), 0.0).astype(BF16)
            stacks = jnp.where(slot_hot, stack_ref[b : b + 1, :].astype(F32), 0.0).astype(BF16)
            hot = hot.astype(BF16)
            table_ref[b * OWN_MAX : (b + 1) * OWN_MAX, :] = (
                dot_nt(fields, hot) * float(LANES) + dot_nt(stacks, hot)
            )
        values_ref[...] = jnp.zeros_like(values_ref)

    table = table_ref[...]
    lane_of = iota((SLOTS, LANES), 1)
    field_of = iota((SLOTS, FIELDS), 1)
    ones = jnp.ones((8, LANES), BF16)
    for i in range(GROUP):
        tile = step * GROUP + i
        block = x_ref[0, :, i * LANES : (i + 1) * LANES]
        blocks_ref[i] = block
        place = jnp.sum(jnp.where(lane_of == tile, table, 0.0), axis=1, keepdims=True).astype(jnp.int32)
        field = lax.shift_right_logical(place, 7)
        lane = lax.bitwise_and(place, LANES - 1)
        rows = dot(jnp.where(field_of == field, 1.0, 0.0).astype(BF16), block)
        picked = jnp.where(lane_of == lane, rows, 0.0).astype(BF16)
        values_ref[pl.ds(tile, 1), 0:SLOTS] = dot_nt(ones, picked)[0:1]

    @pl.when(step == pl.num_programs(0) - 1)
    def _():
        hot, order = owner_order(owner_ref[0:1, :])
        values = values_ref[...]
        turned = values.T[0:OWN_MAX].astype(BF16)
        by_slot = dot(turned, hot.astype(BF16))
        slot_hot = iota((OWN_MAX, OBS), 0).astype(F32) == order
        first = jnp.sum(jnp.where(slot_hot, by_slot, 0.0), axis=0, keepdims=True)
        parts = [
            jnp.broadcast_to(first[:, k * LANES : (k + 1) * LANES][None], (TILES, 1, LANES))
            for k in range(4)
        ]
        parts += [values[:, None, :], jnp.zeros((TILES, 3, LANES), F32)]
        message_ref[...] = jnp.concatenate(parts, axis=1).astype(BF16)


def sort_out(x, owner, field, stack):
    small = pl.BlockSpec((BATCHES, OBS), lambda i: (0, 0))
    return pl.pallas_call(
        sort_out_kernel,
        grid=(TILES // GROUP,),
        in_specs=[pl.BlockSpec((1, FIELDS, GROUP * LANES), lambda i: (0, 0, i)), small, small, small],
        out_specs=[
            pl.BlockSpec((GROUP, FIELDS, LANES), lambda i: (i, 0, 0)),
            pl.BlockSpec((TILES, 8, LANES), lambda i: (0, 0, 0)),
        ],
        out_shape=[
            jax.ShapeDtypeStruct((TILES, FIELDS, LANES), BF16),
            jax.ShapeDtypeStruct((TILES, 8, LANES), BF16),
        ],
        scratch_shapes=[pltpu.VMEM((SLOTS, LANES), F32), pltpu.VMEM((TILES, LANES), F32)],
        compiler_params=pltpu.CompilerParams(vmem_limit_bytes=VMEM_LIMIT),
    )(x, owner, field, stack)


def column(row):
    eye = iota((LANES, LANES), 0) == iota((LANES, LANES), 1)
    return jnp.broadcast_to(
        jnp.sum(jnp.where(eye, row, 0.0), axis=1, keepdims=True), (LANES, LANES)
    )


def lists_kernel(used_ref, owner_ref, roster_ref, kind_ref, reading_ref, variance_ref,
                 weight_ref, observed_ref, noise_ref, listed_ref, slot_ref):
    eye = iota((LANES, LANES), 0) == iota((LANES, LANES), 1)
    for b in range(BATCHES):
        listed = column(roster_ref[b].astype(F32))
        kind = column(kind_ref[b].astype(F32))
        listed_ref[b] = listed.astype(jnp.int32)
        taper = jnp.where(kind > 0.0, (CLASSES + 1 - kind) / CLASSES, 0.0)
        weight_ref[b] = jnp.where(listed < used_ref[b].astype(F32), taper, 0.0)
        _, order = owner_order(owner_ref[b : b + 1, :])
        slot = owner_ref[b : b + 1, :].astype(F32) * OWN_MAX + order
        wide = jnp.concatenate([listed] * (OBS // LANES), axis=1)
        hot = wide == iota((LANES, OBS), 1).astype(F32)

        def look_up(row):
            return jnp.sum(jnp.where(hot, row, 0.0), axis=1, keepdims=True)

        observed_ref[b] = jnp.broadcast_to(look_up(reading_ref[b : b + 1, :]), (LANES, LANES))
        noise_ref[b] = jnp.broadcast_to(look_up(variance_ref[b : b + 1, :]), (LANES, LANES))
        slots = jnp.sum(jnp.where(eye, look_up(slot), 0.0), axis=0, keepdims=True)
        slot_ref[b : b + 1, :] = slots.astype(jnp.int32)


def lists(used, owner, roster, kind, reading, variance):
    vmem = pl.BlockSpec(memory_space=pltpu.VMEM)
    square = jax.ShapeDtypeStruct((BATCHES, LANES, LANES), F32)
    return pl.pallas_call(
        lists_kernel,
        in_specs=[pl.BlockSpec(memory_space=pltpu.SMEM)] + [vmem] * 5,
        out_specs=[vmem] * 5,
        out_shape=[square, square, square, jax.ShapeDtypeStruct(square.shape, jnp.int32),
                   jax.ShapeDtypeStruct((BATCHES, LANES), jnp.int32)],
        compiler_params=pltpu.CompilerParams(vmem_limit_bytes=VMEM_LIMIT),
    )(used, owner, roster, kind, reading, variance)


def transform_of(prior, weight, observed, noise):
    eye = jnp.where(iota((LANES, LANES), 0) == iota((LANES, LANES), 1), 1.0, 0.0)
    mean = jnp.sum(prior, axis=1, keepdims=True) * (1.0 / MEMBERS)
    scaled = weight * (prior - mean) * INVERSE_ROOT
    inverse_noise = 1.0 / noise
    right = jnp.concatenate(
        [scaled * inverse_noise, weight * (observed - mean) * inverse_noise], axis=1
    )
    both = dot(scaled.T, right, HIGHEST)
    matrix = both[:, :LANES] + eye
    pull = both[:, LANES:]
    bound = jnp.max(jnp.sum(jnp.abs(matrix), axis=0, keepdims=True)) * 1.00001
    scale = 2.0 / (1.0 + bound)
    rho = (bound - 1.0) / (bound + 1.0)

    def unfinished(carry):
        return carry[0] > 1e-4

    def square(carry):
        rho, x, e = carry
        gain = 2.0 / (2.0 - rho * rho)
        products = dot(jnp.concatenate([x, e], axis=0), e, HIGHEST)
        x = gain * (x + products[:LANES])
        e = gain * products[LANES:] + (1.0 - gain) * eye
        return rho * rho / (2.0 - rho * rho), x, e

    _, inverse, _ = lax.while_loop(unfinished, square, (rho, scale * eye, eye - scale * matrix))

    def refine(_, x):
        return x + dot(x, eye - dot(matrix, x, HIGHEST), HIGHEST)

    inverse = lax.fori_loop(0, jnp.where(bound > 200.0, 2, 1), refine, inverse)
    return 0.5 * (eye + inverse) + dot(inverse, pull, HIGHEST) * INVERSE_ROOT


def first_kernel(message_ref, listed_ref, weight_ref, observed_ref, noise_ref,
                 sent_ref, own_ref, total_ref, scratch_ref):
    scratch_ref[...] = message_ref[...].astype(F32).reshape(MEMBERS * 8, LANES)
    listed = listed_ref[0]
    prior = jnp.zeros((LANES, MEMBERS), F32)
    for k in range(OBS // LANES):
        values = scratch_ref[pl.ds(k, MEMBERS, stride=8), :].astype(BF16)
        hot = jnp.where(listed == iota((LANES, LANES), 1) + k * LANES, 1.0, 0.0).astype(BF16)
        prior = prior + dot_nt(hot, values)
    own = scratch_ref[pl.ds(4, MEMBERS, stride=8), :].T[0:SLOTS]
    transform = transform_of(prior, weight_ref[0], observed_ref[0], noise_ref[0])
    own = dot(own, transform, HIGHEST)
    own_ref[...] = own
    total_ref[...] = transform
    sent_ref[...] = jnp.broadcast_to(own[OWN_MAX : 2 * OWN_MAX][None], (TILES, OWN_MAX, LANES))


def next_kernel(b, slot_ref, rows_ref, weight_ref, observed_ref, noise_ref, own_ref, total_ref,
                *outs):
    scratch_ref = outs[-1]
    for slot in range(LANES):
        scratch_ref[slot : slot + 1, :] = rows_ref[pl.ds(slot_ref[b, slot], 1), :]
    transform = transform_of(scratch_ref[...], weight_ref[0], observed_ref[0], noise_ref[0])
    if b < BATCHES - 1:
        sent_ref, own_out_ref, total_out_ref = outs[:-1]
        own = dot(own_ref[...], transform, HIGHEST)
        own_out_ref[...] = own
        total_out_ref[...] = dot(total_ref[...], transform, HIGHEST)
        sent = own[(b + 1) * OWN_MAX : (b + 2) * OWN_MAX]
        sent_ref[...] = jnp.broadcast_to(sent[None], (TILES, OWN_MAX, LANES))
    else:
        total = dot(total_ref[...], transform, HIGHEST).T
        high = total.astype(BF16)
        outs[0][:, :LANES] = high
        outs[0][:, LANES:] = (total - high.astype(F32)).astype(BF16)


def solve(b, source, slots, weight, observed, noise, own, total):
    vmem = pl.BlockSpec(memory_space=pltpu.VMEM)
    square = pl.BlockSpec((1, LANES, LANES), lambda i: (b, 0, 0))
    whole = lambda *shape: pl.BlockSpec(shape, lambda i: (0,) * len(shape))
    sent = jax.ShapeDtypeStruct((TILES, OWN_MAX, LANES), F32)
    owned = jax.ShapeDtypeStruct((SLOTS, LANES), F32)
    full = jax.ShapeDtypeStruct((LANES, LANES), F32)
    if b < BATCHES - 1:
        out_shape = [sent, owned, full]
    else:
        out_shape = [jax.ShapeDtypeStruct((LANES, 2 * LANES), BF16)]
    out_specs = [whole(*s.shape) for s in out_shape]
    params = pltpu.CompilerParams(vmem_limit_bytes=VMEM_LIMIT)
    cost = pl.CostEstimate(flops=400_000_000, bytes_accessed=4_000_000, transcendentals=0)
    if b == 0:
        return pl.pallas_call(
            first_kernel,
            grid=(1,),
            in_specs=[whole(MEMBERS, 8, LANES)] + [square] * 4,
            out_specs=out_specs,
            out_shape=out_shape,
            scratch_shapes=[pltpu.VMEM((MEMBERS * 8, LANES), F32)],
            compiler_params=params,
            cost_estimate=cost,
        )(source, slots, weight, observed, noise)
    return pl.pallas_call(
        functools.partial(next_kernel, b),
        grid=(1,),
        in_specs=[pl.BlockSpec(memory_space=pltpu.SMEM), whole(TILES * OWN_MAX, LANES)]
        + [square] * 3
        + [whole(SLOTS, LANES), whole(LANES, LANES)],
        out_specs=out_specs,
        out_shape=out_shape,
        scratch_shapes=[pltpu.VMEM((LANES, LANES), F32)],
        compiler_params=params,
        cost_estimate=cost,
    )(slots, source.reshape(TILES * OWN_MAX, LANES), weight, observed, noise, own, total)


ROWS = 16


def apply_kernel(total_ref, x_ref, out_ref, in_ref, new_ref):
    in_ref[...] = x_ref[...].astype(F32).reshape(MEMBERS * ROWS, LANES)
    total = total_ref[...]
    for v in range(0, ROWS, 2):
        x = jnp.concatenate(
            [in_ref[pl.ds(v + k, MEMBERS, stride=ROWS), :].astype(BF16) for k in range(2)], axis=1
        )
        y = dot(total, jnp.concatenate([x, x], axis=0))
        for k in range(2):
            new_ref[pl.ds(v + k, MEMBERS, stride=ROWS), :] = y[:, k * LANES : (k + 1) * LANES]
    out_ref[...] = new_ref[...].reshape(MEMBERS, ROWS, LANES).astype(BF16)


def apply(total, x):
    block = pl.BlockSpec((MEMBERS, ROWS, LANES), lambda i: (0, i, 0))
    return pl.pallas_call(
        apply_kernel,
        grid=(pl.cdiv(FIELDS, ROWS),),
        in_specs=[pl.BlockSpec((LANES, 2 * LANES), lambda i: (0, 0)), block],
        out_specs=block,
        out_shape=jax.ShapeDtypeStruct((MEMBERS, FIELDS, LANES), BF16),
        scratch_shapes=[pltpu.VMEM((MEMBERS * ROWS, LANES), F32)] * 2,
        compiler_params=pltpu.CompilerParams(vmem_limit_bytes=VMEM_LIMIT),
    )(total, x)


def exchange(x):
    return lax.all_to_all(x, AXES, split_axis=0, concat_axis=0, tiled=False)


def local(
    background_sample,
    measured_reading,
    measurement_noise_variance,
    measurements_in_batch,
    measurement_patch,
    measurement_stack,
    measured_field,
    patch_measurement_roster,
    entry_damping_kind,
):
    owner = measurement_patch.reshape(BATCHES, OBS)
    blocks, message = sort_out(background_sample, owner, measured_field, measurement_stack)
    weight, observed, noise, listed, slots = lists(
        measurements_in_batch, owner, patch_measurement_roster, entry_damping_kind,
        measured_reading, measurement_noise_variance,
    )
    sent, own, total = solve(0, exchange(message), listed, weight, observed, noise, None, None)
    for b in range(1, BATCHES):
        rows = exchange(sent)
        if b == BATCHES - 1:
            rows, blocks = lax.optimization_barrier((rows, blocks))
            (total,) = solve(b, rows, slots, weight, observed, noise, own, total)
        else:
            sent, own, total = solve(b, rows, slots, weight, observed, noise, own, total)
    return apply(total, exchange(blocks))


def solution(mesh):
    in_specs = (
        P(AXES, None, None),
        P(),
        P(),
        P(),
        P(),
        P(),
        P(),
        P(None, AXES, None),
        P(None, AXES, None),
    )
    out_specs = P(None, None, AXES)
    return jax.shard_map(local, mesh=mesh, in_specs=in_specs, out_specs=out_specs, check_vma=False)
```

time: 1450 us -> 256 us (0.18)
  waiting for transfers between devices: 809 us -> 99 us
  local copies, waits for them, and re-layouts: 295 us -> 10.4 us
  other arithmetic: 218 us -> 0 us
  matrix products: 87.9 us -> 0 us
  blocking collectives: 0 us -> 69.6 us
  Pallas kernels: 0 us -> 58.6 us
    all_gather x4 -> x0, waiting for transfers between devices: 725 us -> none  [local(): gathered = lax.all_gather(owned, ('mem', 'tile'), axis=0, tiled=True)]
    unnamed x25 -> x15, local copies, waits for them, and re-layouts: 117 us -> 2.15 us
    unnamed x1 -> x0, other arithmetic: 92.8 us -> none
    another operation x32 -> x0, other arithmetic: 92.4 us -> none  [the longest x12 49.6 us: analyse(): factor = jnp.linalg.cholesky(covariance)]
    dot_general x16 -> x0, matrix products: 84.2 us -> none  [the longest x4 80.1 us: analyse(): jnp.dot(transform.T, spread, precision=lax.Precision.HIGHEST)]
    all_to_all x0 -> x3, blocking collectives: none -> 69.6 us  [exchange(): return lax.all_to_all(x, AXES, split_axis=0, concat_axis=0, tiled=False)]
    pallas_call x0 -> x7, Pallas kernels: none -> 58.6 us  [the longest x1 27.1 us: sort_out(): pl.pallas_call(sort_out_kernel, grid=(TILES // GROUP,), in_specs=[pl.Bloc...]
    convert_element_type x4 -> x0, local copies, waits for them, and re-layouts: 51.3 us -> none  [the longest x2 30.5 us: local(): realization_fields = grouped_per_tile.reshape(realization_number, field_n...]
  transfers between devices with their start and end apart: 5 -> 2, of which waited for: 5 -> 2; matrix products, arithmetic and copies ran while one was open for 3% -> 0% of each run, Pallas kernels for 0% -> 2%
where the time goes in v1:
time: 256 us; the launch traced here: 254 us
  waiting for transfers between devices  99 us (39%)
  blocking collectives  69.6 us (27%)
  Pallas kernels  58.6 us (23%)
  starting transfers between devices  16.3 us (6%)
  local copies, waits for them, and re-layouts  10.4 us (4%)
    all_to_all x2, waiting for transfers between devices, exchange(): return lax.all_to_all(x, AXES, split_axis=0, concat_axis=0, tiled=False)  99 us
    all_to_all x3, blocking collectives, exchange(): return lax.all_to_all(x, AXES, split_axis=0, concat_axis=0, tiled=False)  69.6 us
    pallas_call x1, Pallas kernels, sort_out(): pl.pallas_call(sort_out_kernel, grid=(TILES // GROUP,), in_specs=[pl.Bloc...  27.1 us
    pallas_call x1, Pallas kernels, apply(): pl.pallas_call(apply_kernel, grid=(pl.cdiv(FIELDS, ROWS),), in_specs=[pl....  17 us
    all_to_all x2, starting transfers between devices, exchange(): return lax.all_to_all(x, AXES, split_axis=0, concat_axis=0, tiled=False)  16.3 us
    pallas_call x3, Pallas kernels, solve(): pl.pallas_call(functools.partial(next_kernel, b), grid=(1,), in_specs=[pl...  9.85 us
    pallas_call x1, local copies, waits for them, and re-layouts, apply(): pl.pallas_call(apply_kernel, grid=(pl.cdiv(FIELDS, ROWS),), in_specs=[pl....  8.23 us
  transfers between devices with their start and end apart: 2, of which 2 were waited for; matrix products, arithmetic and copies ran while one was open for 0% of the time, Pallas kernels for 2%

profile of v1, /device:TPU:1, one launch (start us, length us, event | category | flops | bytes accessed | tf_op | source)
XLA Modules:
  0.0 253.9 jit_solution(8840066973546755592)
XLA Ops:
  0.0 0.0 copy-start.6
  0.0 0.0 copy-start.3
  0.0 0.0 copy-start.2
  0.0 0.7 copy.13
  0.7 0.0 copy-start
  0.7 0.7 copy-done
  1.4 0.0 copy-start.1
  1.4 0.7 copy-done.1
  2.1 0.0 copy-start.4
  2.1 0.0 copy-start.5
  2.1 27.1 %shard_map.92 = (bf16[128,227,128]{2,1,0:T(8,128)(2,1)}, bf16[128,8,128]{2,1,0:T(8,128)(2,1)}) custom-call(bf16[1,227,16384]{2,1,0:T(8,128)(2,1)} %x_ref.1, s32[4,512]{1,0:T(4,128)S(1)} %bitcast.9, s32[4,512]{1,0:T(4,128)S(1)} %copy-done, s32[4,512]{1,0:T(4,128)S(1)} %copy-done.1), custom_call_target="tpu_custom_call" | custom-call | tf_op jit(solution)/shard_map/pallas_call | solution.py:97
  29.3 11.5 %all-to-all-start = ((bf16[128,8,128]{2,1,0:T(8,128)(2,1)}), bf16[128,8,128]{2,1,0:T(8,128)(2,1)S(1)}, u32[]{:S(2)}, u32[]{:S(2)}) async-start(bf16[128,8,128]{2,1,0:T(8,128)(2,1)} %get-tuple-element.24), calls=%async_computation | async-start | bytes 524288 | tf_op jit(solution)/shard_map/all_to_all | solution.py:298
  40.8 0.0 copy-done.6
  40.8 0.0 copy-done.3
  40.8 0.0 copy-done.2
  40.8 0.0 copy-done.4
  40.8 0.0 copy-done.5
  40.8 1.4 shard_map.91
  42.2 10.0 %all-to-all-done.message_ref = bf16[128,8,128]{2,1,0:T(8,128)(2,1)S(1)} async-done(((bf16[128,8,128]{2,1,0:T(8,128)(2,1)}), bf16[128,8,128]{2,1,0:T(8,128)(2,1)S(1)}, u32[]{:S(2)}, u32[]{:S(2)}) %all-to-all-start) | async-done | bytes 262176 | tf_op jit(solution)/shard_map/all_to_all | solution.py:298
  52.3 3.2 %shard_map.93 = (f32[128,16,128]{2,1,0:T(8,128)S(1)}, f32[64,128]{1,0:T(8,128)S(1)}, f32[128,128]{1,0:T(8,128)S(1)}) custom-call(bf16[128,8,128]{2,1,0:T(8,128)(2,1)S(1)} %all-to-all-done.message_ref, s32[4,128,128]{2,1,0:T(8,128)S(1)} %get-tuple-element.25.listed_ref, f32[4,128,128]{2,1,0:T(8,128)S(1)} %get-tuple-element.26.weight_ref, ...), custom_call_target="tpu_custom_call" | custom-call | flops 400000000 | bytes 4000000 | tf_op jit(solution)/shard_map/pallas_call | solution.py:244
  55.4 23.1 %all_to_all.25 = f32[128,16,128]{2,1,0:T(8,128)S(1)} all-to-all(f32[128,16,128]{2,1,0:T(8,128)S(1)} %get-tuple-element.29), channel_id=1, replica_groups=mesh['mem'=8,'tile'=16] {'mem','tile'}, dimensions={0} | all-to-all | bytes 2097152 | tf_op jit(solution)/shard_map/all_to_all | solution.py:298
  78.5 3.2 %shard_map.94 = (f32[128,16,128]{2,1,0:T(8,128)S(1)}, f32[64,128]{1,0:T(8,128)S(1)}, f32[128,128]{1,0:T(8,128)S(1)}) custom-call(s32[4,128]{1,0:T(4,128)S(1)} %get-tuple-element.23.slot_ref, f32[2048,128]{1,0:T(8,128)S(1)} %bitcast.7, f32[4,128,128]{2,1,0:T(8,128)S(1)} %get-tuple-element.26.weight_ref, f32[4,128,128]{2,1,0:T(8,128)S(1)} %get-tuple-element.27.observed_ref, ...), custom_call_target="tpu_custom_call" | custom-call | flops 400000000 | bytes 4000000 | tf_op jit(solution)/shard_map/pallas_call | solution.py:254
  81.7 23.4 %all_to_all.26 = f32[128,16,128]{2,1,0:T(8,128)S(1)} all-to-all(f32[128,16,128]{2,1,0:T(8,128)S(1)} %get-tuple-element.32), channel_id=1, replica_groups=mesh['mem'=8,'tile'=16] {'mem','tile'}, dimensions={0} | all-to-all | bytes 2097152 | tf_op jit(solution)/shard_map/all_to_all | solution.py:298
  105.1 3.4 %shard_map.95 = (f32[128,16,128]{2,1,0:T(8,128)S(1)}, f32[64,128]{1,0:T(8,128)S(1)}, f32[128,128]{1,0:T(8,128)S(1)}) custom-call(s32[4,128]{1,0:T(4,128)S(1)} %get-tuple-element.23.slot_ref, f32[2048,128]{1,0:T(8,128)S(1)} %bitcast.8, f32[4,128,128]{2,1,0:T(8,128)S(1)} %get-tuple-element.26.weight_ref, f32[4,128,128]{2,1,0:T(8,128)S(1)} %get-tuple-element.27.observed_ref, ...), custom_call_target="tpu_custom_call" | custom-call | flops 400000000 | bytes 4000000 | tf_op jit(solution)/shard_map/pallas_call | solution.py:254
  108.5 23.1 %all_to_all.27 = f32[128,16,128]{2,1,0:T(8,128)S(1)} all-to-all(f32[128,16,128]{2,1,0:T(8,128)S(1)} %get-tuple-element.35), channel_id=1, replica_groups=mesh['mem'=8,'tile'=16] {'mem','tile'}, dimensions={0} | all-to-all | bytes 2097152 | tf_op jit(solution)/shard_map/all_to_all | solution.py:298
  131.7 4.8 %all-to-all-start.4 = ((bf16[128,227,128]{2,1,0:T(8,128)(2,1)}), bf16[128,227,128]{2,1,0:T(8,128)(2,1)}, u32[]{:S(2)}, u32[]{:S(2)}) async-start(bf16[128,227,128]{2,1,0:T(8,128)(2,1)} %get-tuple-element.40), calls=%async_computation.4 | async-start | bytes 15204352 | tf_op jit(solution)/shard_map/all_to_all | solution.py:298
  136.5 3.2 %shard_map.96.total_ref = bf16[128,256]{1,0:T(8,128)(2,1)S(1)} custom-call(s32[4,128]{1,0:T(4,128)S(1)} %get-tuple-element.23.slot_ref, f32[2048,128]{1,0:T(8,128)S(1)} %bitcast.6, f32[4,128,128]{2,1,0:T(8,128)S(1)} %get-tuple-element.26.weight_ref, f32[4,128,128]{2,1,0:T(8,128)S(1)} %get-tuple-element.27.observed_ref, ...), custom_call_target="tpu_custom_call" | custom-call | flops 400000000 | bytes 4000000 | tf_op jit(solution)/shard_map/pallas_call | solution.py:254
  139.7 88.9 %all-to-all-done.4.x_ref = bf16[128,227,128]{2,1,0:T(8,128)(2,1)} async-done(((bf16[128,227,128]{2,1,0:T(8,128)(2,1)}), bf16[128,227,128]{2,1,0:T(8,128)(2,1)}, u32[]{:S(2)}, u32[]{:S(2)}) %all-to-all-start.4) | async-done | bytes 7438368 | tf_op jit(solution)/shard_map/all_to_all | solution.py:298
  228.7 17.0 %shard_map.97 = bf16[128,227,128]{2,1,0:T(8,128)(2,1)} custom-call(bf16[128,256]{1,0:T(8,128)(2,1)S(1)} %shard_map.96.total_ref, bf16[128,227,128]{2,1,0:T(8,128)(2,1)} %all-to-all-done.4.x_ref), custom_call_target="tpu_custom_call" | custom-call | tf_op jit(solution)/shard_map/pallas_call | solution.py:286
  245.7 8.2 %copy.10 = bf16[128,227,128]{2,0,1:T(8,128)(2,1)} copy(bf16[128,227,128]{2,1,0:T(8,128)(2,1)} %shard_map.97) | data formatting | bytes 14876672 | tf_op jit(solution)/shard_map/pallas_call | solution.py:286
Async XLA Ops:
  0.0 40.8 %copy-start.6 = (s32[4]{0:T(128)S(1)}, s32[4]{0:T(128)}, u32[]{:S(2)}) copy-start(s32[4]{0:T(128)} %used_ref.1) | copy-start | bytes 52
  0.0 40.8 %copy-start.3 = (f32[4,512]{1,0:T(4,128)S(1)}, f32[4,512]{1,0:T(4,128)}, u32[]{:S(2)}) copy-start(f32[4,512]{1,0:T(4,128)} %variance_ref.1) | copy-start | bytes 24580
  0.0 40.8 %copy-start.2 = (f32[4,512]{1,0:T(4,128)S(1)}, f32[4,512]{1,0:T(4,128)}, u32[]{:S(2)}) copy-start(f32[4,512]{1,0:T(4,128)} %reading_ref.1) | copy-start | bytes 24580
  0.7 0.7 copy-start
  1.4 0.7 copy-start.1
  2.1 38.7 %copy-start.4 = (s32[4,1,128]{2,1,0:T(1,128)S(1)}, s32[4,1,128]{2,1,0:T(1,128)}, u32[]{:S(2)}) copy-start(s32[4,1,128]{2,1,0:T(1,128)} %roster_ref.1) | copy-start | bytes 6148
  2.1 38.7 %copy-start.5 = (s32[4,1,128]{2,1,0:T(1,128)S(1)}, s32[4,1,128]{2,1,0:T(1,128)}, u32[]{:S(2)}) copy-start(s32[4,1,128]{2,1,0:T(1,128)} %kind_ref.1) | copy-start | bytes 6148
  29.3 23.0 %all-to-all-start = ((bf16[128,8,128]{2,1,0:T(8,128)(2,1)}), bf16[128,8,128]{2,1,0:T(8,128)(2,1)S(1)}, u32[]{:S(2)}, u32[]{:S(2)}) async-start(bf16[128,8,128]{2,1,0:T(8,128)(2,1)} %get-tuple-element.24), calls=%async_computation | async-start | bytes 524288 | tf_op jit(solution)/shard_map/all_to_all | solution.py:298
  131.7 97.0 %all-to-all-start.4 = ((bf16[128,227,128]{2,1,0:T(8,128)(2,1)}), bf16[128,227,128]{2,1,0:T(8,128)(2,1)}, u32[]{:S(2)}, u32[]{:S(2)}) async-start(bf16[128,227,128]{2,1,0:T(8,128)(2,1)} %get-tuple-element.40), calls=%async_computation.4 | async-start | bytes 15204352 | tf_op jit(solution)/shard_map/all_to_all | solution.py:298

commit v2 on v1

v2 whole, which is shorter than its diff:
```python
import functools
import jax
import jax.numpy as jnp
from jax import lax
from jax.experimental import pallas as pl
from jax.experimental.pallas import tpu as pltpu
from jax.sharding import PartitionSpec as P

OWN_MAX = 16
CLASSES = 8
AXES = ("mem", "tile")
BATCHES = 4
OBS = 512
TILES = 128
MEMBERS = 128
LANES = 128
FIELDS = 227
REST = 3
BULK = FIELDS - REST
SENT = BULK + 8
SLOTS = BATCHES * OWN_MAX
GROUP = 16
PAIRS = TILES // 2
GROUPS = TILES // GROUP
VMEM_LIMIT = 16 * 1024 * 1024
HIGHEST = lax.Precision.HIGHEST
F32 = jnp.float32
BF16 = jnp.bfloat16
INVERSE_ROOT = 1.0 / (MEMBERS - 1) ** 0.5


def iota(shape, dim):
    return lax.broadcasted_iota(jnp.int32, shape, dim)


def dot(a, b, precision=None):
    return jnp.dot(a, b, precision=precision, preferred_element_type=F32)


def dot_nt(a, b):
    return lax.dot_general(a, b, (((1,), (1,)), ((), ())), preferred_element_type=F32)


def owner_orders(owner_ref):
    before = jnp.where(iota((LANES, LANES), 0) < iota((LANES, LANES), 1), 1.0, 0.0).astype(BF16)
    count = jnp.concatenate([before, jnp.ones((LANES, LANES), BF16)], axis=0)
    blocks = OBS // LANES
    hots, rows = [], []
    for b in range(BATCHES):
        hot = jnp.where(iota((TILES, OBS), 0) == owner_ref[b], 1.0, 0.0)
        earlier = jnp.zeros((TILES, LANES), F32)
        for k in range(blocks):
            part = hot[:, k * LANES : (k + 1) * LANES]
            rows.append(jnp.concatenate([part, earlier], axis=1).astype(BF16))
            earlier = earlier + part
        hots.append(hot)
    counts = dot(jnp.concatenate(rows, axis=0), count)
    found = []
    for b, hot in enumerate(hots):
        first = b * blocks * TILES
        wide = jnp.concatenate(
            [counts[first + k * TILES : first + (k + 1) * TILES] for k in range(blocks)], axis=1
        )
        found.append((hot, jnp.sum(hot * wide, axis=0, keepdims=True)))
    return found


def pick_kernel(x_ref, owner_ref, field_ref, stack_ref, message_ref,
                in_ref, new_ref, fields_ref, stacks_ref, values_ref, in_sems, out_sems):
    width = GROUP * LANES
    loads = [
        pltpu.make_async_copy(
            x_ref.at[0, :, pl.ds(i * width, width)], in_ref.at[i], in_sems.at[i]
        )
        for i in range(GROUPS)
    ]
    for load in loads:
        load.start()

    slot_of = lax.bitwise_and(iota((LANES, OBS), 0), SLOTS - 1)
    fields = jnp.zeros((TILES, LANES), F32)
    stacks = jnp.zeros((TILES, LANES), F32)
    orders = owner_orders(owner_ref)
    for b, (hot, order) in enumerate(orders):
        slot_hot = slot_of == order.astype(jnp.int32) + b * OWN_MAX
        hot = hot.astype(BF16)
        of_slot = jnp.where(slot_hot, field_ref[b : b + 1, :].astype(F32), 0.0).astype(BF16)
        fields = fields + dot_nt(hot, of_slot)
        of_slot = jnp.where(slot_hot, stack_ref[b : b + 1, :].astype(F32), 0.0).astype(BF16)
        stacks = stacks + dot_nt(hot, of_slot)
    fields_ref[...] = fields
    stacks_ref[...] = stacks

    left = iota((1, LANES), 1) < SLOTS
    column_of = iota((2 * LANES, LANES), 0).astype(F32).astype(BF16)
    field_of = iota((FIELDS, LANES), 0).astype(F32)
    row_of = iota((8, LANES), 0)
    stores = []
    for group in range(GROUPS):
        loads[group].wait()
        block_ref = in_ref.at[group]
        for i in range(GROUP):
            new_ref[group * GROUP + i, 0:BULK, :] = block_ref[0:BULK, i * LANES : (i + 1) * LANES]
        stores.append(
            pltpu.make_async_copy(
                new_ref.at[pl.ds(group * GROUP, GROUP), pl.ds(0, BULK), :],
                message_ref.at[pl.ds(group * GROUP, GROUP), pl.ds(0, BULK), :],
                out_sems.at[group],
            )
        )
        stores[-1].start()
        for i in range(GROUP // 2):
            tile = group * GROUP + 2 * i
            first, second = stacks_ref[tile : tile + 1, :], stacks_ref[tile + 1 : tile + 2, :]
            column = jnp.where(left, first, second + float(LANES)).astype(BF16)
            hot = jnp.where(column_of == column, jnp.ones((), BF16), jnp.zeros((), BF16))
            by_field = dot(block_ref[:, 2 * i * LANES : (2 * i + 2) * LANES], hot)
            first, second = fields_ref[tile : tile + 1, :], fields_ref[tile + 1 : tile + 2, :]
            field = jnp.where(left, first, second)
            values_ref[tile // 2 : tile // 2 + 1, :] = jnp.sum(
                jnp.where(field_of == field, by_field, 0.0), axis=0, keepdims=True
            )

    order = orders[0][1]
    values = values_ref[...]
    turned = values.T.astype(BF16)
    by_slot = jnp.zeros((OWN_MAX, OBS), F32)
    for k in range(2):
        hot = jnp.where(2 * iota((PAIRS, OBS), 0) + k == owner_ref[0], 1.0, 0.0).astype(BF16)
        by_slot = by_slot + dot(turned[k * SLOTS : k * SLOTS + OWN_MAX], hot)
    slot_hot = iota((OWN_MAX, OBS), 0).astype(F32) == order
    first = jnp.sum(jnp.where(slot_hot, by_slot, 0.0), axis=0, keepdims=True)
    base = jnp.zeros((8, LANES), F32)
    for k in range(OBS // LANES):
        base = jnp.where(row_of == k + REST + 1, first[:, k * LANES : (k + 1) * LANES], base)
    for group in range(GROUPS):
        rest = jnp.concatenate(
            [in_ref[group, BULK:, :].astype(F32), jnp.zeros((8 - REST, width), F32)], axis=0
        )
        for i in range(GROUP):
            tile = group * GROUP + i
            end = jnp.where(
                row_of == REST,
                values[tile // 2 : tile // 2 + 1],
                rest[:, i * LANES : (i + 1) * LANES] + base,
            )
            new_ref[tile, BULK:, :] = end.astype(BF16)
    stores.append(
        pltpu.make_async_copy(
            new_ref.at[:, pl.ds(BULK, 8), :],
            message_ref.at[:, pl.ds(BULK, 8), :],
            out_sems.at[GROUPS],
        )
    )
    stores[-1].start()
    for store in stores:
        store.wait()


def pick(x, owner, field, stack):
    vmem = pl.BlockSpec(memory_space=pltpu.VMEM)
    return pl.pallas_call(
        pick_kernel,
        in_specs=[pl.BlockSpec(memory_space=pl.ANY), vmem, vmem, vmem],
        out_specs=pl.BlockSpec(memory_space=pl.ANY),
        out_shape=jax.ShapeDtypeStruct((TILES, SENT, LANES), BF16),
        scratch_shapes=[
            pltpu.VMEM((GROUPS, FIELDS, GROUP * LANES), BF16),
            pltpu.VMEM((TILES, SENT, LANES), BF16),
            pltpu.VMEM((TILES, LANES), F32),
            pltpu.VMEM((TILES, LANES), F32),
            pltpu.VMEM((PAIRS, LANES), F32),
            pltpu.SemaphoreType.DMA((GROUPS,)),
            pltpu.SemaphoreType.DMA((GROUPS + 1,)),
        ],
        compiler_params=pltpu.CompilerParams(vmem_limit_bytes=63_000_000),
    )(x, owner, field, stack)


def column(row):
    eye = iota((LANES, LANES), 0) == iota((LANES, LANES), 1)
    return jnp.broadcast_to(
        jnp.sum(jnp.where(eye, row, 0.0), axis=1, keepdims=True), (LANES, LANES)
    )


def lists_kernel(used_ref, owner_ref, roster_ref, there_ref, kind_ref, reading_ref, variance_ref,
                 weight_ref, observed_ref, noise_ref, listed_ref, near_ref, slot_ref,
                 slot_there_ref):
    core = lax.rem(lax.axis_index("tile"), 2).astype(F32)
    eye = iota((LANES, LANES), 0) == iota((LANES, LANES), 1)
    for b, (_, order) in enumerate(owner_orders(owner_ref)):
        listed = column(roster_ref[b].astype(F32))
        kind = column(kind_ref[b].astype(F32))
        listed_ref[b] = listed.astype(jnp.int32)
        taper = jnp.where(kind > 0.0, (CLASSES + 1 - kind) / CLASSES, 0.0)
        weight_ref[b] = jnp.where(listed < used_ref[b].astype(F32), taper, 0.0)
        owner = owner_ref[b]
        side = lax.bitwise_and(owner, 1).astype(F32)
        slot = lax.shift_right_logical(owner, 1).astype(F32) * OWN_MAX + order

        def hot_of(listed):
            wide = jnp.concatenate([listed] * (OBS // LANES), axis=1)
            return wide == iota((LANES, OBS), 1).astype(F32)

        hot = hot_of(listed)

        def look_up(row, hot=hot):
            return jnp.sum(jnp.where(hot, row, 0.0), axis=1, keepdims=True)

        def slots(hot):
            row = jnp.sum(jnp.where(eye, look_up(slot, hot), 0.0), axis=0, keepdims=True)
            return row.astype(jnp.int32)

        observed_ref[b] = jnp.broadcast_to(look_up(reading_ref[b : b + 1, :]), (LANES, LANES))
        noise_ref[b] = jnp.broadcast_to(look_up(variance_ref[b : b + 1, :]), (LANES, LANES))
        near_ref[b] = jnp.broadcast_to(
            jnp.where(look_up(side) == core, 1.0, 0.0), (LANES, LANES)
        )
        slot_ref[b : b + 1, :] = slots(hot)
        slot_there_ref[b : b + 1, :] = slots(hot_of(column(there_ref[b].astype(F32))))


def lists(used, owner, roster, there, kind, reading, variance):
    vmem = pl.BlockSpec(memory_space=pltpu.VMEM)
    square = jax.ShapeDtypeStruct((BATCHES, LANES, LANES), F32)
    return pl.pallas_call(
        lists_kernel,
        in_specs=[pl.BlockSpec(memory_space=pltpu.SMEM)] + [vmem] * 6,
        out_specs=[vmem] * 7,
        out_shape=[square, square, square, jax.ShapeDtypeStruct(square.shape, jnp.int32), square,
                   jax.ShapeDtypeStruct((BATCHES, LANES), jnp.int32),
                   jax.ShapeDtypeStruct((BATCHES, LANES), jnp.int32)],
        compiler_params=pltpu.CompilerParams(vmem_limit_bytes=VMEM_LIMIT),
    )(used, owner, roster, there, kind, reading, variance)


def transform_of(prior, weight, observed, noise):
    eye = jnp.where(iota((LANES, LANES), 0) == iota((LANES, LANES), 1), 1.0, 0.0)
    mean = jnp.sum(prior, axis=1, keepdims=True) * (1.0 / MEMBERS)
    scaled = weight * (prior - mean) * INVERSE_ROOT
    inverse_noise = 1.0 / noise
    right = jnp.concatenate(
        [scaled * inverse_noise, weight * (observed - mean) * inverse_noise], axis=1
    )
    both = dot(scaled.T, right, HIGHEST)
    matrix = both[:, :LANES] + eye
    pull = both[:, LANES:]
    bound = jnp.max(jnp.sum(jnp.abs(matrix), axis=0, keepdims=True)) * 1.00001
    scale = 2.0 / (1.0 + bound)
    rho = (bound - 1.0) / (bound + 1.0)

    def unfinished(carry):
        return carry[0] > 3e-4

    def square(carry):
        rho, x, e = carry
        gain = 2.0 / (2.0 - rho * rho)
        products = dot(jnp.concatenate([x, e], axis=0), e, HIGHEST)
        x = gain * (x + products[:LANES])
        e = gain * products[LANES:] + (1.0 - gain) * eye
        return rho * rho / (2.0 - rho * rho), x, e

    _, inverse, _ = lax.while_loop(unfinished, square, (rho, scale * eye, eye - scale * matrix))

    def refine(_, x):
        return x + dot(x, eye - dot(matrix, x, HIGHEST), HIGHEST)

    inverse = lax.fori_loop(0, jnp.where(bound > 200.0, 2, 1), refine, inverse)
    return 0.5 * (eye + inverse) + dot(inverse, pull, HIGHEST) * INVERSE_ROOT


def first_kernel(message_ref, listed_ref, weight_ref, observed_ref, noise_ref,
                 sent_ref, own_ref, total_ref, scratch_ref):
    odd = lax.rem(lax.axis_index("tile"), 2) == 1
    scratch_ref[...] = message_ref[:, 0:8, :].astype(F32).reshape(MEMBERS * 8, LANES)
    listed = listed_ref[0]
    prior = jnp.zeros((LANES, MEMBERS), F32)
    for k in range(OBS // LANES):
        values = scratch_ref[pl.ds(REST + 1 + k, MEMBERS, stride=8), :].astype(BF16)
        hot = jnp.where(listed == iota((LANES, LANES), 1) + k * LANES, 1.0, 0.0).astype(BF16)
        prior = prior + dot_nt(hot, values)
    pair = scratch_ref[pl.ds(REST, MEMBERS, stride=8), :].T
    own = jnp.where(odd, pair[SLOTS:], pair[:SLOTS])
    transform = transform_of(prior, weight_ref[0], observed_ref[0], noise_ref[0])
    own = dot(own, transform, HIGHEST)
    own_ref[...] = own
    total_ref[...] = transform
    sent_ref[...] = jnp.broadcast_to(own[OWN_MAX : 2 * OWN_MAX][None], (PAIRS, OWN_MAX, LANES))


def next_kernel(b, near_ref, far_ref, side_ref, weight_ref, observed_ref, noise_ref, own_ref,
                total_ref, *outs):
    prior = jnp.where(side_ref[0] > 0.0, near_ref[...], far_ref[...])
    transform = transform_of(prior, weight_ref[0], observed_ref[0], noise_ref[0])
    if b < BATCHES - 1:
        sent_ref, own_out_ref, total_out_ref = outs
        own = dot(own_ref[...], transform, HIGHEST)
        own_out_ref[...] = own
        total_out_ref[...] = dot(total_ref[...], transform, HIGHEST)
        sent = own[(b + 1) * OWN_MAX : (b + 2) * OWN_MAX]
        sent_ref[...] = jnp.broadcast_to(sent[None], (PAIRS, OWN_MAX, LANES))
    else:
        total = dot(total_ref[...], transform, HIGHEST).T
        high = total.astype(BF16)
        outs[0][:, :LANES] = high
        outs[0][:, LANES:] = (total - high.astype(F32)).astype(BF16)


def whole(*shape):
    return pl.BlockSpec(shape, lambda i: (0,) * len(shape))


def solve(b, near, far, lists_of, own=None, total=None):
    weight, observed, noise, listed, side = lists_of[:5]
    square = pl.BlockSpec((1, LANES, LANES), lambda i: (b, 0, 0))
    sent = jax.ShapeDtypeStruct((PAIRS, OWN_MAX, LANES), F32)
    owned = jax.ShapeDtypeStruct((SLOTS, LANES), F32)
    full = jax.ShapeDtypeStruct((LANES, LANES), F32)
    if b < BATCHES - 1:
        out_shape = [sent, owned, full]
    else:
        out_shape = [jax.ShapeDtypeStruct((LANES, 2 * LANES), BF16)]
    out_specs = [whole(*s.shape) for s in out_shape]
    params = pltpu.CompilerParams(vmem_limit_bytes=VMEM_LIMIT)
    cost = pl.CostEstimate(flops=400_000_000, bytes_accessed=4_000_000, transcendentals=0)
    if b == 0:
        return pl.pallas_call(
            first_kernel,
            grid=(1,),
            in_specs=[pl.BlockSpec((MEMBERS, 16, LANES), lambda i: (0, BULK // 16, 0))] + [square] * 4,
            out_specs=out_specs,
            out_shape=out_shape,
            scratch_shapes=[pltpu.VMEM((MEMBERS * 8, LANES), F32)],
            compiler_params=params,
            cost_estimate=cost,
        )(near, listed, weight, observed, noise)
    return pl.pallas_call(
        functools.partial(next_kernel, b),
        grid=(1,),
        in_specs=[whole(LANES, LANES)] * 2
        + [square] * 4
        + [whole(SLOTS, LANES), whole(LANES, LANES)],
        out_specs=out_specs,
        out_shape=out_shape,
        compiler_params=params,
        cost_estimate=cost,
    )(near, far, side, weight, observed, noise, own, total)


def select_kernel(b, slot_ref, rows_ref, out_ref):
    for slot in range(LANES):
        out_ref[slot : slot + 1, :] = rows_ref[pl.ds(slot_ref[b, slot], 1), :]


def select(b, slots, rows):
    return pl.pallas_call(
        functools.partial(select_kernel, b),
        grid=(1,),
        in_specs=[pl.BlockSpec(memory_space=pltpu.SMEM), whole(PAIRS * OWN_MAX, LANES)],
        out_specs=whole(LANES, LANES),
        out_shape=jax.ShapeDtypeStruct((LANES, LANES), F32),
        compiler_params=pltpu.CompilerParams(vmem_limit_bytes=VMEM_LIMIT),
        cost_estimate=pl.CostEstimate(flops=0, bytes_accessed=1_000_000, transcendentals=0),
    )(slots, rows)


ROWS = 32
CHUNKS = BULK // ROWS


def turn_kernel(end_ref, x_ref, out_ref, in_ref, flat_ref, sems):
    loads = [
        pltpu.make_async_copy(x_ref.at[:, pl.ds(i * ROWS, ROWS), :], in_ref.at[i], sems.at[i])
        for i in range(CHUNKS)
    ]
    for load in loads:
        load.start()
    flat_ref[:, 0:8, :] = end_ref[:, 0:8, :].astype(F32)
    rows_ref = flat_ref.reshape(MEMBERS * (ROWS + 8), LANES)

    def row(v):
        return rows_ref[pl.ds(v, MEMBERS, stride=ROWS + 8), :].astype(BF16)

    for k in range(REST):
        out_ref[BULK + k] = row(k)
    for k in range(FIELDS, SENT):
        out_ref[k] = jnp.zeros((MEMBERS, LANES), BF16)
    for i in range(CHUNKS):
        loads[i].wait()
        flat_ref[:, 0:ROWS, :] = in_ref[i].astype(F32)
        for v in range(ROWS):
            out_ref[i * ROWS + v] = row(v)


def turn(x):
    return pl.pallas_call(
        turn_kernel,
        in_specs=[
            pl.BlockSpec((MEMBERS, 16, LANES), lambda i: (0, BULK // 16, 0)),
            pl.BlockSpec(memory_space=pl.ANY),
        ],
        grid=(1,),
        out_specs=whole(SENT, MEMBERS, LANES),
        out_shape=jax.ShapeDtypeStruct((SENT, MEMBERS, LANES), BF16),
        scratch_shapes=[
            pltpu.VMEM((CHUNKS, MEMBERS, ROWS, LANES), BF16),
            pltpu.VMEM((MEMBERS, ROWS + 8, LANES), F32),
            pltpu.SemaphoreType.DMA((CHUNKS,)),
        ],
        compiler_params=pltpu.CompilerParams(vmem_limit_bytes=30 * 1024 * 1024),
        cost_estimate=pl.CostEstimate(flops=0, bytes_accessed=15_000_000, transcendentals=0),
    )(x, x)


STEP = SENT // 4


def apply_kernel(total_ref, x_ref, out_ref):
    total = total_ref[...]
    first = pl.program_id(0) * STEP
    for v in range(0, STEP, 2):
        x = jnp.concatenate([x_ref[first + v], x_ref[first + v + 1]], axis=1)
        y = dot(total, jnp.concatenate([x, x], axis=0)).astype(BF16)
        for k in range(2):
            out_ref[v + k] = y[:, k * LANES : (k + 1) * LANES]


def apply(total, x):
    return pl.pallas_call(
        apply_kernel,
        grid=(SENT // STEP,),
        in_specs=[whole(LANES, 2 * LANES), pl.BlockSpec(memory_space=pltpu.VMEM)],
        out_specs=pl.BlockSpec((STEP, MEMBERS, LANES), lambda i: (i, 0, 0)),
        out_shape=jax.ShapeDtypeStruct((FIELDS, MEMBERS, LANES), BF16),
        compiler_params=pltpu.CompilerParams(vmem_limit_bytes=30 * 1024 * 1024),
    )(total, x)


def exchange(x, groups=None):
    return lax.all_to_all(x, AXES, split_axis=0, concat_axis=0, axis_index_groups=groups)


def to_chips(x):
    return exchange(x, [list(range(core, TILES, 2)) for core in range(2)])


def swap(x):
    size = lax.axis_size("tile")
    return lax.ppermute(x, "tile", [(i, i ^ 1) for i in range(size)])


def local(
    background_sample,
    measured_reading,
    measurement_noise_variance,
    measurements_in_batch,
    measurement_patch,
    measurement_stack,
    measured_field,
    patch_measurement_roster,
    entry_damping_kind,
):
    owner = measurement_patch.reshape(BATCHES, 1, OBS)
    roster_there = swap(patch_measurement_roster)
    message = pick(background_sample, owner, measured_field, measurement_stack)
    message, used = lax.optimization_barrier((message, measurements_in_batch))
    lists_of = lists(
        used, owner, patch_measurement_roster, roster_there, entry_damping_kind,
        measured_reading, measurement_noise_variance,
    )
    fields, lists_of = lax.optimization_barrier((exchange(message), lists_of))
    slots, slots_there = lists_of[-2:]
    sent, own, total = solve(0, fields, None, lists_of)
    sent, fields_later = lax.optimization_barrier((sent, fields))
    for b in range(1, BATCHES):
        rows = to_chips(sent).reshape(PAIRS * OWN_MAX, LANES)
        if b == 1:
            rows, turned = lax.optimization_barrier((rows, turn(fields_later)))
        far = swap(select(b, slots_there, rows))
        near = select(b, slots, rows)
        if b == BATCHES - 1:
            (total,) = solve(b, near, far, lists_of, own, total)
        else:
            sent, own, total = solve(b, near, far, lists_of, own, total)
    return apply(total, turned).transpose(1, 0, 2)


def solution(mesh):
    in_specs = (
        P(AXES, None, None),
        P(),
        P(),
        P(),
        P(),
        P(),
        P(),
        P(None, AXES, None),
        P(None, AXES, None),
    )
    out_specs = P(None, None, AXES)
    return jax.shard_map(local, mesh=mesh, in_specs=in_specs, out_specs=out_specs, check_vma=False)
```

time: 256 us -> 195 us (0.76)
  blocking collectives: 69.6 us -> 33.9 us
  Pallas kernels: 58.6 us -> 35.6 us
  starting transfers between devices: 16.3 us -> 28.8 us
  local copies, waits for them, and re-layouts: 10.4 us -> 3.03 us
  waiting for transfers between devices: 99 us -> 93.3 us
    all_to_all x3 -> x2, blocking collectives: 69.6 us -> 33.9 us  [exchange(): lax.all_to_all(x, AXES, split_axis=0, concat_axis=0, axis_index_groups=gr...]
    pallas_call x6 -> x13, Pallas kernels: 57.2 us -> 34 us  [the longest x3 7.83 us: solve(): pl.pallas_call(functools.partial(next_kernel, b), grid=(1,), in_specs=[wh...]
    pallas_call x1 -> x0, local copies, waits for them, and re-layouts: 8.23 us -> none  [apply(): pl.pallas_call(apply_kernel, grid=(pl.cdiv(FIELDS, ROWS),), in_specs=[pl....]
    ppermute x0 -> x4, starting transfers between devices: none -> 7.47 us  [swap(): return lax.ppermute(x, 'tile', [(i, i ^ 1) for i in range(size)])]
    all_to_all x2, waiting for transfers between devices: 99 us -> 91.7 us  [exchange(): lax.all_to_all(x, AXES, split_axis=0, concat_axis=0, axis_index_groups=gr...]
    all_to_all x2, starting transfers between devices: 16.3 us -> 21.3 us  [exchange(): lax.all_to_all(x, AXES, split_axis=0, concat_axis=0, axis_index_groups=gr...]
  transfers between devices with their start and end apart: 2 -> 6, of which waited for: 2 -> 6; matrix products, arithmetic and copies ran while one was open for 0% -> 0% of each run, Pallas kernels for 2% -> 5%
where the time goes in v2:
time: 195 us
  waiting for transfers between devices  93.3 us (48%)
  Pallas kernels  35.6 us (18%)
  blocking collectives  33.9 us (17%)
  starting transfers between devices  28.8 us (15%)
  local copies, waits for them, and re-layouts  3.03 us (2%)
    all_to_all x2, waiting for transfers between devices, exchange(): lax.all_to_all(x, AXES, split_axis=0, concat_axis=0, axis_index_groups=gr...  91.7 us
    all_to_all x2, blocking collectives, exchange(): lax.all_to_all(x, AXES, split_axis=0, concat_axis=0, axis_index_groups=gr...  33.9 us
    all_to_all x2, starting transfers between devices, exchange(): lax.all_to_all(x, AXES, split_axis=0, concat_axis=0, axis_index_groups=gr...  21.3 us
    pallas_call x3, Pallas kernels, solve(): pl.pallas_call(functools.partial(next_kernel, b), grid=(1,), in_specs=[wh...  7.83 us
    pallas_call x1, Pallas kernels, pick(): pl.pallas_call(pick_kernel, in_specs=[pl.BlockSpec(memory_space=pl.ANY),...  7.55 us
    ppermute x4, starting transfers between devices, swap(): return lax.ppermute(x, 'tile', [(i, i ^ 1) for i in range(size)])  7.47 us
    pallas_call x1, Pallas kernels, turn(): pl.pallas_call(turn_kernel, in_specs=[pl.BlockSpec((MEMBERS, 16, LANES),...  5.41 us
    pallas_call x1, Pallas kernels, solve(): pl.pallas_call(first_kernel, grid=(1,), in_specs=[pl.BlockSpec((MEMBERS,...  4.9 us
  transfers between devices with their start and end apart: 6, of which 6 were waited for; matrix products, arithmetic and copies ran while one was open for 0% of the time, Pallas kernels for 5%

profile of v2, /device:TPU:1, one launch (start us, length us, event | category | flops | bytes accessed | tf_op | source)
XLA Modules:
  0.0 194.9 jit_solution(1587126771522928368)
XLA Ops:
  0.0 7.5 %shard_map.91 = bf16[128,232,128]{2,1,0:T(8,128)(2,1)} custom-call(bf16[1,227,16384]{2,1,0:T(8,128)(2,1)} %x_ref.1, s32[4,1,512]{2,1,0:T(1,128)} %bitcast.11, s32[4,512]{1,0:T(4,128)} %field_ref.1, s32[4,512]{1,0:T(4,128)} %stack_ref.1), custom_call_target="tpu_custom_call" | custom-call | tf_op jit(solution)/shard_map/pallas_call | solution.py:162
  7.6 0.0 copy-start.2
  7.6 0.0 copy-start.3
  7.6 0.0 copy-start.7
  7.6 11.9 %all-to-all-start = ((bf16[128,232,128]{2,1,0:T(8,128)(2,1)}), bf16[128,232,128]{2,1,0:T(8,128)(2,1)}, u32[]{:S(2)}, u32[]{:S(2)}) async-start(bf16[128,232,128]{2,1,0:T(8,128)(2,1)} %shard_map.91), calls=%async_computation | async-start | bytes 15204352 | tf_op jit(solution)/shard_map/all_to_all | solution.py:441
  19.5 1.2 collective-permute-start
  20.8 0.8 collective-permute-done.there_ref
  21.6 1.7 shard_map.92
  23.3 88.3 %all-to-all-done.message_ref.end_ref.x_ref = bf16[128,232,128]{2,1,0:T(8,128)(2,1)} async-done(((bf16[128,232,128]{2,1,0:T(8,128)(2,1)}), bf16[128,232,128]{2,1,0:T(8,128)(2,1)}, u32[]{:S(2)}, u32[]{:S(2)}) %all-to-all-start) | async-done | bytes 7602208 | tf_op jit(solution)/shard_map/all_to_all | solution.py:441
  111.6 4.9 %shard_map.93 = (f32[64,16,128]{2,1,0:T(8,128)}, f32[64,128]{1,0:T(8,128)S(1)}, f32[128,128]{1,0:T(8,128)S(1)}) custom-call(bf16[128,232,128]{2,1,0:T(8,128)(2,1)} %all-to-all-done.message_ref.end_ref.x_ref, s32[4,128,128]{2,1,0:T(8,128)S(1)} %get-tuple-element.46.listed_ref, f32[4,128,128]{2,1,0:T(8,128)S(1)} %get-tuple-element.47.weight_ref, ...), custom_call_target="tpu_custom_call" | custom-call | flops 400000000 | bytes 4000000 | tf_op jit(solution)/shard_map/pallas_call | solution.py:328
  116.5 9.4 %all-to-all-start.1 = ((f32[64,16,128]{2,1,0:T(8,128)}), f32[64,16,128]{2,1,0:T(8,128)S(1)}, u32[]{:S(2)}, u32[]{:S(2)}) async-start(f32[64,16,128]{2,1,0:T(8,128)} %get-tuple-element.51), calls=%async_computation.1 | async-start | bytes 1048576 | tf_op jit(solution)/shard_map/all_to_all | solution.py:441
  125.9 5.4 %shard_map.94.x_ref = bf16[232,128,128]{2,1,0:T(8,128)(2,1)S(1)} custom-call(bf16[128,232,128]{2,1,0:T(8,128)(2,1)} %all-to-all-done.message_ref.end_ref.x_ref, bf16[128,232,128]{2,1,0:T(8,128)(2,1)} %all-to-all-done.message_ref.end_ref.x_ref), custom_call_target="tpu_custom_call" | custom-call | bytes 15000000 | tf_op jit(solution)/shard_map/pallas_call | solution.py:397
  131.3 3.0 %copy-done = bf16[232,128,128]{2,1,0:T(8,128)(2,1)} copy-done((bf16[232,128,128]{2,1,0:T(8,128)(2,1)}, bf16[232,128,128]{2,1,0:T(8,128)(2,1)S(1)}, u32[]{:S(2)}) %copy-start) | copy-done | bytes 7602200
  134.3 3.4 %all-to-all-done.1 = f32[64,16,128]{2,1,0:T(8,128)S(1)} async-done(((f32[64,16,128]{2,1,0:T(8,128)}), f32[64,16,128]{2,1,0:T(8,128)S(1)}, u32[]{:S(2)}, u32[]{:S(2)}) %all-to-all-start.1) | async-done | bytes 524320 | tf_op jit(solution)/shard_map/all_to_all | solution.py:441
  137.7 0.6 shard_map.96
  138.4 2.3 %collective-permute-start.1 = (f32[128,128]{1,0:T(8,128)S(1)}, f32[128,128]{1,0:T(8,128)S(1)}, u32[]{:S(2)}, u32[]{:S(2)}) collective-permute-start(f32[128,128]{1,0:T(8,128)S(1)} %shard_map.96), channel_id=1, source_target_pairs={{0,1},{1,0},{2,3},{3,2},{4,5},{5,4},{6,7},{7,6},{8,9},{9,8},{10,11... | collective-permute-start | bytes 196616 | tf_op jit(solution)/shard_map/ppermute | solution.py:450
  140.7 0.6 shard_map.95.near_ref
  141.3 0.3 collective-permute-done.1.far_ref
  141.6 2.8 %shard_map.97 = (f32[64,16,128]{2,1,0:T(8,128)S(1)}, f32[64,128]{1,0:T(8,128)S(1)}, f32[128,128]{1,0:T(8,128)S(1)}) custom-call(f32[128,128]{1,0:T(8,128)S(1)} %shard_map.95.near_ref, f32[128,128]{1,0:T(8,128)S(1)} %collective-permute-done.1.far_ref, f32[4,128,128]{2,1,0:T(8,128)S(1)} %get-tuple-element.55.side_ref, ...), custom_call_target="tpu_custom_call" | custom-call | flops 400000000 | bytes 4000000 | tf_op jit(solution)/shard_map/pallas_call | solution.py:338
  144.3 17.7 %all_to_all.20 = f32[64,16,128]{2,1,0:T(8,128)S(1)} all-to-all(f32[64,16,128]{2,1,0:T(8,128)S(1)} %get-tuple-element.58), channel_id=1, replica_groups={{0,2,4,6,8,10,12,14,16,18,20,22,24,26,28,30,32,34,36,38,40,42,44,46,48,..., dimensions={0} | all-to-all | bytes 1048576 | tf_op jit(solution)/shard_map/all_to_all | solution.py:441
  162.0 0.6 shard_map.99
  162.6 1.8 collective-permute-start.2
  164.4 0.6 shard_map.98.near_ref
  165.0 0.3 collective-permute-done.2.far_ref
  165.3 2.5 %shard_map.100 = (f32[64,16,128]{2,1,0:T(8,128)S(1)}, f32[64,128]{1,0:T(8,128)S(1)}, f32[128,128]{1,0:T(8,128)S(1)}) custom-call(f32[128,128]{1,0:T(8,128)S(1)} %shard_map.98.near_ref, f32[128,128]{1,0:T(8,128)S(1)} %collective-permute-done.2.far_ref, f32[4,128,128]{2,1,0:T(8,128)S(1)} %get-tuple-element.55.side_ref, ...), custom_call_target="tpu_custom_call" | custom-call | flops 400000000 | bytes 4000000 | tf_op jit(solution)/shard_map/pallas_call | solution.py:338
  167.8 16.3 %all_to_all.21 = f32[64,16,128]{2,1,0:T(8,128)S(1)} all-to-all(f32[64,16,128]{2,1,0:T(8,128)S(1)} %get-tuple-element.61), channel_id=1, replica_groups={{0,2,4,6,8,10,12,14,16,18,20,22,24,26,28,30,32,34,36,38,40,42,44,46,48,..., dimensions={0} | all-to-all | bytes 1048576 | tf_op jit(solution)/shard_map/all_to_all | solution.py:441
  184.1 0.6 shard_map.102
  184.7 2.2 %collective-permute-start.3 = (f32[128,128]{1,0:T(8,128)S(1)}, f32[128,128]{1,0:T(8,128)S(1)}, u32[]{:S(2)}, u32[]{:S(2)}) collective-permute-start(f32[128,128]{1,0:T(8,128)S(1)} %shard_map.102), channel_id=1, source_target_pairs={{0,1},{1,0},{2,3},{3,2},{4,5},{5,4},{6,7},{7,6},{8,9},{9,8},{10,11... | collective-permute-start | bytes 196616 | tf_op jit(solution)/shard_map/ppermute | solution.py:450
  186.9 0.6 shard_map.101.near_ref
  187.6 0.3 collective-permute-done.3.far_ref
  187.8 2.6 %shard_map.103.total_ref = bf16[128,256]{1,0:T(8,128)(2,1)S(1)} custom-call(f32[128,128]{1,0:T(8,128)S(1)} %shard_map.101.near_ref, f32[128,128]{1,0:T(8,128)S(1)} %collective-permute-done.3.far_ref, f32[4,128,128]{2,1,0:T(8,128)S(1)} %get-tuple-element.55.side_ref, f32[4,128,128]{2,1,0:T(8,128)S(1)} %get-tuple-element.47.weight_ref, ...), custom_call_target="tpu_custom_call" | custom-call | flops 400000000 | bytes 4000000 | tf_op jit(solution)/shard_map/pallas_call | solution.py:338
  190.4 4.5 %shard_map.104 = bf16[227,128,128]{2,1,0:T(8,128)(2,1)} custom-call(bf16[128,256]{1,0:T(8,128)(2,1)S(1)} %shard_map.103.total_ref, bf16[232,128,128]{2,1,0:T(8,128)(2,1)S(1)} %copy-done.1), custom_call_target="tpu_custom_call" | custom-call | tf_op jit(solution)/shard_map/pallas_call | solution.py:430
  (12 shorter events, 0.0 us)
Async XLA Ops:
  7.6 12.0 %copy-start.5 = (s32[4,1,128]{2,1,0:T(1,128)S(1)}, s32[4,1,128]{2,1,0:T(1,128)}, u32[]{:S(2)}) copy-start(s32[4,1,128]{2,1,0:T(1,128)} %roster_ref.1) | copy-start | bytes 6148
  7.6 14.0 %copy-start.2 = (s32[4,512,1]{1,2,0:T(1,128)S(1)}, s32[4,512,1]{1,2,0:T(1,128)}, u32[]{:S(2)}) copy-start(s32[4,512,1]{1,2,0:T(1,128)} %param.13) | copy-start | bytes 24580
  7.6 14.0 %copy-start.3 = (f32[4,512]{1,0:T(4,128)S(1)}, f32[4,512]{1,0:T(4,128)}, u32[]{:S(2)}) copy-start(f32[4,512]{1,0:T(4,128)} %reading_ref.1) | copy-start | bytes 24580
  7.6 14.0 %copy-start.4 = (f32[4,512]{1,0:T(4,128)S(1)}, f32[4,512]{1,0:T(4,128)}, u32[]{:S(2)}) copy-start(f32[4,512]{1,0:T(4,128)} %variance_ref.1) | copy-start | bytes 24580
  7.6 14.0 %copy-start.6 = (s32[4,1,128]{2,1,0:T(1,128)S(1)}, s32[4,1,128]{2,1,0:T(1,128)}, u32[]{:S(2)}) copy-start(s32[4,1,128]{2,1,0:T(1,128)} %kind_ref.1) | copy-start | bytes 6148
  7.6 14.0 %copy-start.7 = (s32[4]{0:T(128)S(1)}, s32[4]{0:T(128)}, u32[]{:S(2)}) copy-start(s32[4]{0:T(128)} %used_ref) | copy-start | bytes 52
  7.6 104.0 %all-to-all-start = ((bf16[128,232,128]{2,1,0:T(8,128)(2,1)}), bf16[128,232,128]{2,1,0:T(8,128)(2,1)}, u32[]{:S(2)}, u32[]{:S(2)}) async-start(bf16[128,232,128]{2,1,0:T(8,128)(2,1)} %shard_map.91), calls=%async_computation | async-start | bytes 15204352 | tf_op jit(solution)/shard_map/all_to_all | solution.py:441
  19.5 2.0 %collective-permute-start = (s32[4,1,128]{2,1,0:T(1,128)S(1)}, s32[4,1,128]{2,1,0:T(1,128)S(1)}, u32[]{:S(2)}, u32[]{:S(2)}) collective-permute-start(s32[4,1,128]{2,1,0:T(1,128)S(1)} %copy-done.5), channel_id=1, source_target_pairs={{0,1},{1,0},{2,3},{3,2},{4,5},{5,4},{6,7},{7,6},{8,9},{9,8},{10,11... | collective-permute-start | bytes 6152 | tf_op jit(solution)/shard_map/ppermute | solution.py:450
  116.5 21.2 %all-to-all-start.1 = ((f32[64,16,128]{2,1,0:T(8,128)}), f32[64,16,128]{2,1,0:T(8,128)S(1)}, u32[]{:S(2)}, u32[]{:S(2)}) async-start(f32[64,16,128]{2,1,0:T(8,128)} %get-tuple-element.51), calls=%async_computation.1 | async-start | bytes 1048576 | tf_op jit(solution)/shard_map/all_to_all | solution.py:441
  131.3 3.0 %copy-start = (bf16[232,128,128]{2,1,0:T(8,128)(2,1)}, bf16[232,128,128]{2,1,0:T(8,128)(2,1)S(1)}, u32[]{:S(2)}) copy-start(bf16[232,128,128]{2,1,0:T(8,128)(2,1)S(1)} %shard_map.94.x_ref) | copy-start | bytes 22806532
  137.7 52.7 %copy-start.1 = (bf16[232,128,128]{2,1,0:T(8,128)(2,1)S(1)}, bf16[232,128,128]{2,1,0:T(8,128)(2,1)}, u32[]{:S(2)}) copy-start(bf16[232,128,128]{2,1,0:T(8,128)(2,1)} %copy-done) | copy-start | bytes 22806532
  138.4 3.2 %collective-permute-start.1 = (f32[128,128]{1,0:T(8,128)S(1)}, f32[128,128]{1,0:T(8,128)S(1)}, u32[]{:S(2)}, u32[]{:S(2)}) collective-permute-start(f32[128,128]{1,0:T(8,128)S(1)} %shard_map.96), channel_id=1, source_target_pairs={{0,1},{1,0},{2,3},{3,2},{4,5},{5,4},{6,7},{7,6},{8,9},{9,8},{10,11... | collective-permute-start | bytes 196616 | tf_op jit(solution)/shard_map/ppermute | solution.py:450
  162.6 2.7 %collective-permute-start.2 = (f32[128,128]{1,0:T(8,128)S(1)}, f32[128,128]{1,0:T(8,128)S(1)}, u32[]{:S(2)}, u32[]{:S(2)}) collective-permute-start(f32[128,128]{1,0:T(8,128)S(1)} %shard_map.99), channel_id=1, source_target_pairs={{0,1},{1,0},{2,3},{3,2},{4,5},{5,4},{6,7},{7,6},{8,9},{9,8},{10,11... | collective-permute-start | bytes 196616 | tf_op jit(solution)/shard_map/ppermute | solution.py:450
  184.7 3.1 %collective-permute-start.3 = (f32[128,128]{1,0:T(8,128)S(1)}, f32[128,128]{1,0:T(8,128)S(1)}, u32[]{:S(2)}, u32[]{:S(2)}) collective-permute-start(f32[128,128]{1,0:T(8,128)S(1)} %shard_map.102), channel_id=1, source_target_pairs={{0,1},{1,0},{2,3},{3,2},{4,5},{5,4},{6,7},{7,6},{8,9},{9,8},{10,11... | collective-permute-start | bytes 196616 | tf_op jit(solution)/shard_map/ppermute | solution.py:450

commit v3 on v2

--- a/solution.py
+++ b/solution.py
@@ -25,6 +25,8 @@
 VMEM_LIMIT = 16 * 1024 * 1024
 HIGHEST = lax.Precision.HIGHEST
 F32 = jnp.float32
+FINEST = 0.25
+CODES_PER_OCTAVE = 1326.0
 BF16 = jnp.bfloat16
 INVERSE_ROOT = 1.0 / (MEMBERS - 1) ** 0.5
 
@@ -235,6 +237,16 @@
     )(used, owner, roster, there, kind, reading, variance)
 
 
+def coded(x):
+    size = CODES_PER_OCTAVE * jnp.log2(1.0 + jnp.abs(x) * (1.0 / FINEST))
+    return jnp.round(jnp.where(x < 0.0, -size, size)).astype(jnp.int32).astype(jnp.int16)
+
+
+def decoded(code):
+    size = jnp.exp2(jnp.abs(code) * (1.0 / CODES_PER_OCTAVE)) - 1.0
+    return jnp.where(code < 0.0, -FINEST, FINEST) * size
+
+
 def transform_of(prior, weight, observed, noise):
     eye = jnp.where(iota((LANES, LANES), 0) == iota((LANES, LANES), 1), 1.0, 0.0)
     mean = jnp.sum(prior, axis=1, keepdims=True) * (1.0 / MEMBERS)
@@ -256,7 +268,7 @@
     def square(carry):
         rho, x, e = carry
         gain = 2.0 / (2.0 - rho * rho)
-        products = dot(jnp.concatenate([x, e], axis=0), e, HIGHEST)
+        products = dot(jnp.concatenate([x, e], axis=0), e, lax.Precision.HIGH)
         x = gain * (x + products[:LANES])
         e = gain * products[LANES:] + (1.0 - gain) * eye
         return rho * rho / (2.0 - rho * rho), x, e
@@ -275,23 +287,37 @@
     odd = lax.rem(lax.axis_index("tile"), 2) == 1
     scratch_ref[...] = message_ref[:, 0:8, :].astype(F32).reshape(MEMBERS * 8, LANES)
     listed = listed_ref[0]
-    prior = jnp.zeros((LANES, MEMBERS), F32)
-    for k in range(OBS // LANES):
-        values = scratch_ref[pl.ds(REST + 1 + k, MEMBERS, stride=8), :].astype(BF16)
-        hot = jnp.where(listed == iota((LANES, LANES), 1) + k * LANES, 1.0, 0.0).astype(BF16)
-        prior = prior + dot_nt(hot, values)
+    values = jnp.concatenate(
+        [
+            scratch_ref[pl.ds(REST + 1 + k, MEMBERS, stride=8), :].astype(BF16)
+            for k in range(OBS // LANES)
+        ],
+        axis=1,
+    )
+    hot = jnp.concatenate(
+        [
+            jnp.where(listed == iota((LANES, LANES), 1) + k * LANES, 1.0, 0.0).astype(BF16)
+            for k in range(OBS // LANES)
+        ],
+        axis=1,
+    )
+    prior = dot_nt(hot, values)
     pair = scratch_ref[pl.ds(REST, MEMBERS, stride=8), :].T
     own = jnp.where(odd, pair[SLOTS:], pair[:SLOTS])
     transform = transform_of(prior, weight_ref[0], observed_ref[0], noise_ref[0])
     own = dot(own, transform, HIGHEST)
     own_ref[...] = own
     total_ref[...] = transform
-    sent_ref[...] = jnp.broadcast_to(own[OWN_MAX : 2 * OWN_MAX][None], (PAIRS, OWN_MAX, LANES))
+    sent_ref[...] = jnp.broadcast_to(
+        coded(own[OWN_MAX : 2 * OWN_MAX])[None], (PAIRS, OWN_MAX, LANES)
+    )
 
 
 def next_kernel(b, near_ref, far_ref, side_ref, weight_ref, observed_ref, noise_ref, own_ref,
                 total_ref, *outs):
-    prior = jnp.where(side_ref[0] > 0.0, near_ref[...], far_ref[...])
+    near = near_ref[...].astype(jnp.int32).astype(F32)
+    far = far_ref[...].astype(jnp.int32).astype(F32)
+    prior = decoded(jnp.where(side_ref[0] > 0.0, near, far))
     transform = transform_of(prior, weight_ref[0], observed_ref[0], noise_ref[0])
     if b < BATCHES - 1:
         sent_ref, own_out_ref, total_out_ref = outs
@@ -299,7 +325,7 @@
         own_out_ref[...] = own
         total_out_ref[...] = dot(total_ref[...], transform, HIGHEST)
         sent = own[(b + 1) * OWN_MAX : (b + 2) * OWN_MAX]
-        sent_ref[...] = jnp.broadcast_to(sent[None], (PAIRS, OWN_MAX, LANES))
+        sent_ref[...] = jnp.broadcast_to(coded(sent)[None], (PAIRS, OWN_MAX, LANES))
     else:
         total = dot(total_ref[...], transform, HIGHEST).T
         high = total.astype(BF16)
@@ -314,7 +340,7 @@
 def solve(b, near, far, lists_of, own=None, total=None):
     weight, observed, noise, listed, side = lists_of[:5]
     square = pl.BlockSpec((1, LANES, LANES), lambda i: (b, 0, 0))
-    sent = jax.ShapeDtypeStruct((PAIRS, OWN_MAX, LANES), F32)
+    sent = jax.ShapeDtypeStruct((PAIRS, OWN_MAX, LANES), jnp.int16)
     owned = jax.ShapeDtypeStruct((SLOTS, LANES), F32)
     full = jax.ShapeDtypeStruct((LANES, LANES), F32)
     if b < BATCHES - 1:
@@ -348,9 +374,11 @@
     )(near, far, side, weight, observed, noise, own, total)
 
 
-def select_kernel(b, slot_ref, rows_ref, out_ref):
+def select_kernel(b, slot_ref, rows_ref, out_ref, wide_ref, found_ref):
+    wide_ref[...] = rows_ref[...].astype(jnp.int32)
     for slot in range(LANES):
-        out_ref[slot : slot + 1, :] = rows_ref[pl.ds(slot_ref[b, slot], 1), :]
+        found_ref[slot : slot + 1, :] = wide_ref[pl.ds(slot_ref[b, slot], 1), :]
+    out_ref[...] = found_ref[...].astype(jnp.int16)
 
 
 def select(b, slots, rows):
@@ -359,7 +387,11 @@
         grid=(1,),
         in_specs=[pl.BlockSpec(memory_space=pltpu.SMEM), whole(PAIRS * OWN_MAX, LANES)],
         out_specs=whole(LANES, LANES),
-        out_shape=jax.ShapeDtypeStruct((LANES, LANES), F32),
+        out_shape=jax.ShapeDtypeStruct((LANES, LANES), jnp.int16),
+        scratch_shapes=[
+            pltpu.VMEM((PAIRS * OWN_MAX, LANES), jnp.int32),
+            pltpu.VMEM((LANES, LANES), jnp.int32),
+        ],
         compiler_params=pltpu.CompilerParams(vmem_limit_bytes=VMEM_LIMIT),
         cost_estimate=pl.CostEstimate(flops=0, bytes_accessed=1_000_000, transcendentals=0),
     )(slots, rows)
@@ -369,71 +401,64 @@
 CHUNKS = BULK // ROWS
 
 
-def turn_kernel(end_ref, x_ref, out_ref, in_ref, flat_ref, sems):
+def apply_kernel(total_ref, x_ref, out_ref, in_ref, end_ref, new_ref, flat_ref, in_sems, out_sems):
     loads = [
-        pltpu.make_async_copy(x_ref.at[:, pl.ds(i * ROWS, ROWS), :], in_ref.at[i], sems.at[i])
+        pltpu.make_async_copy(x_ref.at[:, pl.ds(i * ROWS, ROWS), :], in_ref.at[i], in_sems.at[i])
         for i in range(CHUNKS)
     ]
+    loads.append(
+        pltpu.make_async_copy(x_ref.at[:, pl.ds(BULK, 8), :], end_ref, in_sems.at[CHUNKS])
+    )
     for load in loads:
         load.start()
-    flat_ref[:, 0:8, :] = end_ref[:, 0:8, :].astype(F32)
+    total = total_ref[...]
     rows_ref = flat_ref.reshape(MEMBERS * (ROWS + 8), LANES)
 
     def row(v):
         return rows_ref[pl.ds(v, MEMBERS, stride=ROWS + 8), :].astype(BF16)
 
-    for k in range(REST):
-        out_ref[BULK + k] = row(k)
-    for k in range(FIELDS, SENT):
-        out_ref[k] = jnp.zeros((MEMBERS, LANES), BF16)
-    for i in range(CHUNKS):
+    def transformed(x):
+        return dot(total, jnp.concatenate([x, x], axis=0)).astype(BF16)
+
+    stores = []
+    for i in range(CHUNKS + 1):
         loads[i].wait()
-        flat_ref[:, 0:ROWS, :] = in_ref[i].astype(F32)
-        for v in range(ROWS):
-            out_ref[i * ROWS + v] = row(v)
-
-
-def turn(x):
-    return pl.pallas_call(
-        turn_kernel,
-        in_specs=[
-            pl.BlockSpec((MEMBERS, 16, LANES), lambda i: (0, BULK // 16, 0)),
-            pl.BlockSpec(memory_space=pl.ANY),
-        ],
-        grid=(1,),
-        out_specs=whole(SENT, MEMBERS, LANES),
-        out_shape=jax.ShapeDtypeStruct((SENT, MEMBERS, LANES), BF16),
-        scratch_shapes=[
-            pltpu.VMEM((CHUNKS, MEMBERS, ROWS, LANES), BF16),
-            pltpu.VMEM((MEMBERS, ROWS + 8, LANES), F32),
-            pltpu.SemaphoreType.DMA((CHUNKS,)),
-        ],
-        compiler_params=pltpu.CompilerParams(vmem_limit_bytes=30 * 1024 * 1024),
-        cost_estimate=pl.CostEstimate(flops=0, bytes_accessed=15_000_000, transcendentals=0),
-    )(x, x)
-
-
-STEP = SENT // 4
-
-
-def apply_kernel(total_ref, x_ref, out_ref):
-    total = total_ref[...]
-    first = pl.program_id(0) * STEP
-    for v in range(0, STEP, 2):
-        x = jnp.concatenate([x_ref[first + v], x_ref[first + v + 1]], axis=1)
-        y = dot(total, jnp.concatenate([x, x], axis=0)).astype(BF16)
-        for k in range(2):
-            out_ref[v + k] = y[:, k * LANES : (k + 1) * LANES]
+        number = ROWS if i < CHUNKS else REST
+        if i < CHUNKS:
+            flat_ref[:, 0:ROWS, :] = in_ref[i].astype(F32)
+        else:
+            flat_ref[:, 0:8, :] = end_ref[...].astype(F32)
+        for v in range(0, number, 2):
+            y = transformed(jnp.concatenate([row(v), row(v + 1)], axis=1))
+            for k in range(min(2, number - v)):
+                new_ref[i * ROWS + v + k] = y[:, k * LANES : (k + 1) * LANES]
+        places = pl.ds(i * ROWS, number)
+        stores.append(
+            pltpu.make_async_copy(new_ref.at[places], out_ref.at[places], out_sems.at[i])
+        )
+        stores[-1].start()
+    for store in stores:
+        store.wait()
 
 
 def apply(total, x):
     return pl.pallas_call(
         apply_kernel,
-        grid=(SENT // STEP,),
-        in_specs=[whole(LANES, 2 * LANES), pl.BlockSpec(memory_space=pltpu.VMEM)],
-        out_specs=pl.BlockSpec((STEP, MEMBERS, LANES), lambda i: (i, 0, 0)),
+        in_specs=[
+            pl.BlockSpec(memory_space=pltpu.VMEM),
+            pl.BlockSpec(memory_space=pl.ANY),
+        ],
+        out_specs=pl.BlockSpec(memory_space=pl.ANY),
         out_shape=jax.ShapeDtypeStruct((FIELDS, MEMBERS, LANES), BF16),
-        compiler_params=pltpu.CompilerParams(vmem_limit_bytes=30 * 1024 * 1024),
+        scratch_shapes=[
+            pltpu.VMEM((CHUNKS, MEMBERS, ROWS, LANES), BF16),
+            pltpu.VMEM((MEMBERS, 8, LANES), BF16),
+            pltpu.VMEM((FIELDS, MEMBERS, LANES), BF16),
+            pltpu.VMEM((MEMBERS, ROWS + 8, LANES), F32),
+            pltpu.SemaphoreType.DMA((CHUNKS + 1,)),
+            pltpu.SemaphoreType.DMA((CHUNKS + 1,)),
+        ],
+        compiler_params=pltpu.CompilerParams(vmem_limit_bytes=60_000_000),
     )(total, x)
 
 
@@ -472,18 +497,15 @@
     fields, lists_of = lax.optimization_barrier((exchange(message), lists_of))
     slots, slots_there = lists_of[-2:]
     sent, own, total = solve(0, fields, None, lists_of)
-    sent, fields_later = lax.optimization_barrier((sent, fields))
     for b in range(1, BATCHES):
         rows = to_chips(sent).reshape(PAIRS * OWN_MAX, LANES)
-        if b == 1:
-            rows, turned = lax.optimization_barrier((rows, turn(fields_later)))
         far = swap(select(b, slots_there, rows))
         near = select(b, slots, rows)
         if b == BATCHES - 1:
             (total,) = solve(b, near, far, lists_of, own, total)
         else:
             sent, own, total = solve(b, near, far, lists_of, own, total)
-    return apply(total, turned).transpose(1, 0, 2)
+    return apply(total, fields).transpose(1, 0, 2)
 
 
 def solution(mesh):

time: 195 us -> 189 us (0.969)
  blocking collectives: 33.9 us -> 47.1 us
  starting transfers between devices: 28.8 us -> 18.9 us
  waiting for transfers between devices: 93.3 us -> 89.6 us
  Pallas kernels: 35.6 us -> 32.5 us
  local copies, waits for them, and re-layouts: 3.03 us -> 0.65 us
    all_to_all x2 -> x3, blocking collectives: 33.9 us -> 47.1 us  [exchange(): lax.all_to_all(x, AXES, split_axis=0, concat_axis=0, axis_index_groups=gr...]
    all_to_all x2 -> x1, starting transfers between devices: 21.3 us -> 11.9 us  [exchange(): lax.all_to_all(x, AXES, split_axis=0, concat_axis=0, axis_index_groups=gr...]
    all_to_all x2 -> x1, waiting for transfers between devices: 91.7 us -> 88.3 us  [exchange(): lax.all_to_all(x, AXES, split_axis=0, concat_axis=0, axis_index_groups=gr...]
    unnamed x16 -> x14, local copies, waits for them, and re-layouts: 3.03 us -> 0.65 us
    pallas_call x2 -> x1, Pallas kernels: 9.91 us -> 8.18 us  [apply(): pl.pallas_call(apply_kernel, in_specs=[pl.BlockSpec(memory_space=pltpu.VM...]
  transfers between devices with their start and end apart: 6 -> 5, of which waited for: 6 -> 5; matrix products, arithmetic and copies ran while one was open for 0% -> 0% of each run, Pallas kernels for 5% -> 2%
where the time goes in v3:
time: 189 us
  waiting for transfers between devices  89.6 us (47%)
  blocking collectives  47.1 us (25%)
  Pallas kernels  32.5 us (17%)
  starting transfers between devices  18.9 us (10%)
    all_to_all x1, waiting for transfers between devices, exchange(): lax.all_to_all(x, AXES, split_axis=0, concat_axis=0, axis_index_groups=gr...  88.3 us
    all_to_all x3, blocking collectives, exchange(): lax.all_to_all(x, AXES, split_axis=0, concat_axis=0, axis_index_groups=gr...  47.1 us
    all_to_all x1, starting transfers between devices, exchange(): lax.all_to_all(x, AXES, split_axis=0, concat_axis=0, axis_index_groups=gr...  11.9 us
    pallas_call x1, Pallas kernels, apply(): pl.pallas_call(apply_kernel, in_specs=[pl.BlockSpec(memory_space=pltpu.VM...  8.18 us
    pallas_call x1, Pallas kernels, pick(): pl.pallas_call(pick_kernel, in_specs=[pl.BlockSpec(memory_space=pl.ANY),...  7.57 us
    pallas_call x3, Pallas kernels, solve(): pl.pallas_call(functools.partial(next_kernel, b), grid=(1,), in_specs=[wh...  7.21 us
    ppermute x4, starting transfers between devices, swap(): return lax.ppermute(x, 'tile', [(i, i ^ 1) for i in range(size)])  7 us
    pallas_call x6, Pallas kernels, select(): pl.pallas_call(functools.partial(select_kernel, b), grid=(1,), in_specs=[...  4.19 us
  transfers between devices with their start and end apart: 5, of which 5 were waited for; matrix products, arithmetic and copies ran while one was open for 0% of the time, Pallas kernels for 2%

profile of v3, /device:TPU:1, one launch (start us, length us, event | category | flops | bytes accessed | tf_op | source)
XLA Modules:
  0.0 189.1 jit_solution(9482771153575245300)
XLA Ops:
  0.0 7.6 %shard_map.91 = bf16[128,232,128]{2,1,0:T(8,128)(2,1)} custom-call(bf16[1,227,16384]{2,1,0:T(8,128)(2,1)} %x_ref.1, s32[4,1,512]{2,1,0:T(1,128)} %bitcast.11, s32[4,512]{1,0:T(4,128)} %field_ref.1, s32[4,512]{1,0:T(4,128)} %stack_ref.1), custom_call_target="tpu_custom_call" | custom-call | tf_op jit(solution)/shard_map/pallas_call | solution.py:164
  7.6 0.0 copy-start.4
  7.6 0.0 copy-start.1
  7.6 0.0 copy-start.2
  7.6 0.0 copy-start.5
  7.6 0.0 copy-start.6
  7.7 11.9 %all-to-all-start = ((bf16[128,232,128]{2,1,0:T(8,128)(2,1)}), bf16[128,232,128]{2,1,0:T(8,128)(2,1)}, u32[]{:S(2)}, u32[]{:S(2)}) async-start(bf16[128,232,128]{2,1,0:T(8,128)(2,1)} %shard_map.91), calls=%async_computation | async-start | bytes 15204352 | tf_op jit(solution)/shard_map/all_to_all | solution.py:466
  19.6 1.2 collective-permute-start
  20.8 0.8 collective-permute-done.there_ref
  21.6 1.7 shard_map.92
  23.3 88.3 %all-to-all-done.message_ref.x_ref = bf16[128,232,128]{2,1,0:T(8,128)(2,1)} async-done(((bf16[128,232,128]{2,1,0:T(8,128)(2,1)}), bf16[128,232,128]{2,1,0:T(8,128)(2,1)}, u32[]{:S(2)}, u32[]{:S(2)}) %all-to-all-start) | async-done | bytes 7602208 | tf_op jit(solution)/shard_map/all_to_all | solution.py:466
  111.6 3.7 %shard_map.93 = (s16[64,16,128]{2,1,0:T(8,128)(2,1)S(1)}, f32[64,128]{1,0:T(8,128)S(1)}, f32[128,128]{1,0:T(8,128)S(1)}) custom-call(bf16[128,232,128]{2,1,0:T(8,128)(2,1)} %all-to-all-done.message_ref.x_ref, s32[4,128,128]{2,1,0:T(8,128)S(1)} %get-tuple-element.42.listed_ref, f32[4,128,128]{2,1,0:T(8,128)S(1)} %get-tuple-element.43.weight_ref, ...), custom_call_target="tpu_custom_call" | custom-call | flops 400000000 | bytes 4000000 | tf_op jit(solution)/shard_map/pallas_call | solution.py:354
  115.3 18.5 %all_to_all.20 = s16[64,16,128]{2,1,0:T(8,128)(2,1)S(1)} all-to-all(s16[64,16,128]{2,1,0:T(8,128)(2,1)S(1)} %get-tuple-element.46), channel_id=1, replica_groups={{0,2,4,6,8,10,12,14,16,18,20,22,24,26,28,30,32,34,36,38,40,42,44,46,48,..., dimensions={0} | all-to-all | bytes 524288 | tf_op jit(solution)/shard_map/all_to_all | solution.py:466
  133.8 0.7 shard_map.95
  134.5 2.2 %collective-permute-start.1 = (s16[128,128]{1,0:T(8,128)(2,1)S(1)}, s16[128,128]{1,0:T(8,128)(2,1)S(1)}, u32[]{:S(2)}, u32[]{:S(2)}) collective-permute-start(s16[128,128]{1,0:T(8,128)(2,1)S(1)} %shard_map.95), channel_id=1, source_target_pairs={{0,1},{1,0},{2,3},{3,2},{4,5},{5,4},{6,7},{7,6},{8,9},{9,8},{10,11... | collective-permute-start | bytes 98312 | tf_op jit(solution)/shard_map/ppermute | solution.py:475
  136.7 0.7 shard_map.94.near_ref
  137.4 0.2 collective-permute-done.1.far_ref
  137.6 2.5 %shard_map.96 = (s16[64,16,128]{2,1,0:T(8,128)(2,1)S(1)}, f32[64,128]{1,0:T(8,128)S(1)}, f32[128,128]{1,0:T(8,128)S(1)}) custom-call(s16[128,128]{1,0:T(8,128)(2,1)S(1)} %shard_map.94.near_ref, s16[128,128]{1,0:T(8,128)(2,1)S(1)} %collective-permute-done.1.far_ref, f32[4,128,128]{2,1,0:T(8,128)S(1)} %get-tuple-element.48.side_ref, ...), custom_call_target="tpu_custom_call" | custom-call | flops 400000000 | bytes 4000000 | tf_op jit(solution)/shard_map/pallas_call | solution.py:364
  140.1 14.2 %all_to_all.21 = s16[64,16,128]{2,1,0:T(8,128)(2,1)S(1)} all-to-all(s16[64,16,128]{2,1,0:T(8,128)(2,1)S(1)} %get-tuple-element.51), channel_id=1, replica_groups={{0,2,4,6,8,10,12,14,16,18,20,22,24,26,28,30,32,34,36,38,40,42,44,46,48,..., dimensions={0} | all-to-all | bytes 524288 | tf_op jit(solution)/shard_map/all_to_all | solution.py:466
  154.3 0.7 shard_map.98
  155.0 1.9 %collective-permute-start.2 = (s16[128,128]{1,0:T(8,128)(2,1)S(1)}, s16[128,128]{1,0:T(8,128)(2,1)S(1)}, u32[]{:S(2)}, u32[]{:S(2)}) collective-permute-start(s16[128,128]{1,0:T(8,128)(2,1)S(1)} %shard_map.98), channel_id=1, source_target_pairs={{0,1},{1,0},{2,3},{3,2},{4,5},{5,4},{6,7},{7,6},{8,9},{9,8},{10,11... | collective-permute-start | bytes 98312 | tf_op jit(solution)/shard_map/ppermute | solution.py:475
  156.9 0.7 shard_map.97.near_ref
  157.6 0.2 collective-permute-done.2.far_ref
  157.7 2.3 %shard_map.99 = (s16[64,16,128]{2,1,0:T(8,128)(2,1)S(1)}, f32[64,128]{1,0:T(8,128)S(1)}, f32[128,128]{1,0:T(8,128)S(1)}) custom-call(s16[128,128]{1,0:T(8,128)(2,1)S(1)} %shard_map.97.near_ref, s16[128,128]{1,0:T(8,128)(2,1)S(1)} %collective-permute-done.2.far_ref, f32[4,128,128]{2,1,0:T(8,128)S(1)} %get-tuple-element.48.side_ref, ...), custom_call_target="tpu_custom_call" | custom-call | flops 400000000 | bytes 4000000 | tf_op jit(solution)/shard_map/pallas_call | solution.py:364
  160.0 14.4 %all_to_all.22 = s16[64,16,128]{2,1,0:T(8,128)(2,1)S(1)} all-to-all(s16[64,16,128]{2,1,0:T(8,128)(2,1)S(1)} %get-tuple-element.54), channel_id=1, replica_groups={{0,2,4,6,8,10,12,14,16,18,20,22,24,26,28,30,32,34,36,38,40,42,44,46,48,..., dimensions={0} | all-to-all | bytes 524288 | tf_op jit(solution)/shard_map/all_to_all | solution.py:466
  174.4 0.7 shard_map.101
  175.2 1.7 collective-permute-start.3
  176.9 0.7 shard_map.100.near_ref
  177.6 0.2 collective-permute-done.3.far_ref
  177.7 2.4 %shard_map.102.total_ref = bf16[128,256]{1,0:T(8,128)(2,1)S(1)} custom-call(s16[128,128]{1,0:T(8,128)(2,1)S(1)} %shard_map.100.near_ref, s16[128,128]{1,0:T(8,128)(2,1)S(1)} %collective-permute-done.3.far_ref, f32[4,128,128]{2,1,0:T(8,128)S(1)} %get-tuple-element.48.side_ref, f32[4,128,128]{2,1,0:T(8,128)S(1)} %get-tuple-element.43.weight_ref, ...), custom_call_target="tpu_custom_call" | custom-call | flops 400000000 | bytes 4000000 | tf_op jit(solution)/shard_map/pallas_call | solution.py:364
  180.1 0.6 copy-done
  180.7 8.2 %shard_map.103 = bf16[227,128,128]{2,1,0:T(8,128)(2,1)} custom-call(bf16[128,256]{1,0:T(8,128)(2,1)} %copy-done, bf16[128,232,128]{2,1,0:T(8,128)(2,1)} %all-to-all-done.message_ref.x_ref), custom_call_target="tpu_custom_call" | custom-call | tf_op jit(solution)/shard_map/pallas_call | solution.py:445
  (8 shorter events, 0.0 us)
Async XLA Ops:
  7.6 12.0 %copy-start.4 = (s32[4,1,128]{2,1,0:T(1,128)S(1)}, s32[4,1,128]{2,1,0:T(1,128)}, u32[]{:S(2)}) copy-start(s32[4,1,128]{2,1,0:T(1,128)} %roster_ref.1) | copy-start | bytes 6148
  7.6 14.0 %copy-start.1 = (s32[4,512,1]{1,2,0:T(1,128)S(1)}, s32[4,512,1]{1,2,0:T(1,128)}, u32[]{:S(2)}) copy-start(s32[4,512,1]{1,2,0:T(1,128)} %param.13) | copy-start | bytes 24580
  7.6 14.0 %copy-start.2 = (f32[4,512]{1,0:T(4,128)S(1)}, f32[4,512]{1,0:T(4,128)}, u32[]{:S(2)}) copy-start(f32[4,512]{1,0:T(4,128)} %reading_ref.1) | copy-start | bytes 24580
  7.6 14.0 %copy-start.3 = (f32[4,512]{1,0:T(4,128)S(1)}, f32[4,512]{1,0:T(4,128)}, u32[]{:S(2)}) copy-start(f32[4,512]{1,0:T(4,128)} %variance_ref.1) | copy-start | bytes 24580
  7.6 14.0 %copy-start.5 = (s32[4,1,128]{2,1,0:T(1,128)S(1)}, s32[4,1,128]{2,1,0:T(1,128)}, u32[]{:S(2)}) copy-start(s32[4,1,128]{2,1,0:T(1,128)} %kind_ref.1) | copy-start | bytes 6148
  7.6 14.0 %copy-start.6 = (s32[4]{0:T(128)S(1)}, s32[4]{0:T(128)}, u32[]{:S(2)}) copy-start(s32[4]{0:T(128)} %used_ref) | copy-start | bytes 52
  7.7 104.0 %all-to-all-start = ((bf16[128,232,128]{2,1,0:T(8,128)(2,1)}), bf16[128,232,128]{2,1,0:T(8,128)(2,1)}, u32[]{:S(2)}, u32[]{:S(2)}) async-start(bf16[128,232,128]{2,1,0:T(8,128)(2,1)} %shard_map.91), calls=%async_computation | async-start | bytes 15204352 | tf_op jit(solution)/shard_map/all_to_all | solution.py:466
  19.6 2.0 %collective-permute-start = (s32[4,1,128]{2,1,0:T(1,128)S(1)}, s32[4,1,128]{2,1,0:T(1,128)S(1)}, u32[]{:S(2)}, u32[]{:S(2)}) collective-permute-start(s32[4,1,128]{2,1,0:T(1,128)S(1)} %copy-done.4), channel_id=1, source_target_pairs={{0,1},{1,0},{2,3},{3,2},{4,5},{5,4},{6,7},{7,6},{8,9},{9,8},{10,11... | collective-permute-start | bytes 6152 | tf_op jit(solution)/shard_map/ppermute | solution.py:475
  134.5 3.0 %collective-permute-start.1 = (s16[128,128]{1,0:T(8,128)(2,1)S(1)}, s16[128,128]{1,0:T(8,128)(2,1)S(1)}, u32[]{:S(2)}, u32[]{:S(2)}) collective-permute-start(s16[128,128]{1,0:T(8,128)(2,1)S(1)} %shard_map.95), channel_id=1, source_target_pairs={{0,1},{1,0},{2,3},{3,2},{4,5},{5,4},{6,7},{7,6},{8,9},{9,8},{10,11... | collective-permute-start | bytes 98312 | tf_op jit(solution)/shard_map/ppermute | solution.py:475
  155.0 2.8 %collective-permute-start.2 = (s16[128,128]{1,0:T(8,128)(2,1)S(1)}, s16[128,128]{1,0:T(8,128)(2,1)S(1)}, u32[]{:S(2)}, u32[]{:S(2)}) collective-permute-start(s16[128,128]{1,0:T(8,128)(2,1)S(1)} %shard_map.98), channel_id=1, source_target_pairs={{0,1},{1,0},{2,3},{3,2},{4,5},{5,4},{6,7},{7,6},{8,9},{9,8},{10,11... | collective-permute-start | bytes 98312 | tf_op jit(solution)/shard_map/ppermute | solution.py:475
  175.2 2.6 %collective-permute-start.3 = (s16[128,128]{1,0:T(8,128)(2,1)S(1)}, s16[128,128]{1,0:T(8,128)(2,1)S(1)}, u32[]{:S(2)}, u32[]{:S(2)}) collective-permute-start(s16[128,128]{1,0:T(8,128)(2,1)S(1)} %shard_map.101), channel_id=1, source_target_pairs={{0,1},{1,0},{2,3},{3,2},{4,5},{5,4},{6,7},{7,6},{8,9},{9,8},{10,11... | collective-permute-start | bytes 98312 | tf_op jit(solution)/shard_map/ppermute | solution.py:475
  180.1 0.6 copy-start

commit v4 on v3

--- a/solution.py
+++ b/solution.py
@@ -283,7 +283,7 @@
 
 
 def first_kernel(message_ref, listed_ref, weight_ref, observed_ref, noise_ref,
-                 sent_ref, own_ref, total_ref, scratch_ref):
+                 sent_ref, total_ref, own_ref, scratch_ref):
     odd = lax.rem(lax.axis_index("tile"), 2) == 1
     scratch_ref[...] = message_ref[:, 0:8, :].astype(F32).reshape(MEMBERS * 8, LANES)
     listed = listed_ref[0]
@@ -303,75 +303,78 @@
     )
     prior = dot_nt(hot, values)
     pair = scratch_ref[pl.ds(REST, MEMBERS, stride=8), :].T
-    own = jnp.where(odd, pair[SLOTS:], pair[:SLOTS])
+    own = jnp.where(odd, pair[SLOTS + OWN_MAX :], pair[OWN_MAX:SLOTS])
     transform = transform_of(prior, weight_ref[0], observed_ref[0], noise_ref[0])
     own = dot(own, transform, HIGHEST)
-    own_ref[...] = own
+    own_ref[...] = own[OWN_MAX:]
     total_ref[...] = transform
     sent_ref[...] = jnp.broadcast_to(
-        coded(own[OWN_MAX : 2 * OWN_MAX])[None], (PAIRS, OWN_MAX, LANES)
-    )
-
-
-def next_kernel(b, near_ref, far_ref, side_ref, weight_ref, observed_ref, noise_ref, own_ref,
-                total_ref, *outs):
+        coded(own[:OWN_MAX])[None], (PAIRS, OWN_MAX, LANES)
+    )
+
+
+def prior_of(side_ref, near_ref, far_ref):
     near = near_ref[...].astype(jnp.int32).astype(F32)
     far = far_ref[...].astype(jnp.int32).astype(F32)
-    prior = decoded(jnp.where(side_ref[0] > 0.0, near, far))
+    return decoded(jnp.where(side_ref[0] > 0.0, near, far))
+
+
+def next_kernel(near_ref, far_ref, side_ref, weight_ref, observed_ref, noise_ref, own_ref,
+                total_ref, sent_ref, total_out_ref, *rest_ref):
+    prior = prior_of(side_ref, near_ref, far_ref)
     transform = transform_of(prior, weight_ref[0], observed_ref[0], noise_ref[0])
-    if b < BATCHES - 1:
-        sent_ref, own_out_ref, total_out_ref = outs
-        own = dot(own_ref[...], transform, HIGHEST)
-        own_out_ref[...] = own
-        total_out_ref[...] = dot(total_ref[...], transform, HIGHEST)
-        sent = own[(b + 1) * OWN_MAX : (b + 2) * OWN_MAX]
-        sent_ref[...] = jnp.broadcast_to(coded(sent)[None], (PAIRS, OWN_MAX, LANES))
-    else:
-        total = dot(total_ref[...], transform, HIGHEST).T
-        high = total.astype(BF16)
-        outs[0][:, :LANES] = high
-        outs[0][:, LANES:] = (total - high.astype(F32)).astype(BF16)
+    left = own_ref.shape[0]
+    new = dot(jnp.concatenate([own_ref[...], total_ref[...]], axis=0), transform, HIGHEST)
+    sent_ref[...] = jnp.broadcast_to(coded(new[:OWN_MAX])[None], (PAIRS, OWN_MAX, LANES))
+    if left > OWN_MAX:
+        rest_ref[0][...] = new[OWN_MAX:left]
+    total_out_ref[...] = new[left:]
 
 
 def whole(*shape):
     return pl.BlockSpec(shape, lambda i: (0,) * len(shape))
 
 
+def list_blocks(b, number):
+    return [pl.BlockSpec((1, LANES, LANES), lambda i: (b, 0, 0))] * number
+
+
 def solve(b, near, far, lists_of, own=None, total=None):
     weight, observed, noise, listed, side = lists_of[:5]
-    square = pl.BlockSpec((1, LANES, LANES), lambda i: (b, 0, 0))
-    sent = jax.ShapeDtypeStruct((PAIRS, OWN_MAX, LANES), jnp.int16)
-    owned = jax.ShapeDtypeStruct((SLOTS, LANES), F32)
-    full = jax.ShapeDtypeStruct((LANES, LANES), F32)
-    if b < BATCHES - 1:
-        out_shape = [sent, owned, full]
-    else:
-        out_shape = [jax.ShapeDtypeStruct((LANES, 2 * LANES), BF16)]
-    out_specs = [whole(*s.shape) for s in out_shape]
+    left = (BATCHES - 2 - b) * OWN_MAX
+    out_shape = [
+        jax.ShapeDtypeStruct((PAIRS, OWN_MAX, LANES), jnp.int16),
+        jax.ShapeDtypeStruct((LANES, LANES), F32),
+    ]
+    if left:
+        out_shape.append(jax.ShapeDtypeStruct((left, LANES), F32))
     params = pltpu.CompilerParams(vmem_limit_bytes=VMEM_LIMIT)
     cost = pl.CostEstimate(flops=400_000_000, bytes_accessed=4_000_000, transcendentals=0)
     if b == 0:
-        return pl.pallas_call(
-            first_kernel,
-            grid=(1,),
-            in_specs=[pl.BlockSpec((MEMBERS, 16, LANES), lambda i: (0, BULK // 16, 0))] + [square] * 4,
-            out_specs=out_specs,
-            out_shape=out_shape,
-            scratch_shapes=[pltpu.VMEM((MEMBERS * 8, LANES), F32)],
-            compiler_params=params,
-            cost_estimate=cost,
-        )(near, listed, weight, observed, noise)
-    return pl.pallas_call(
-        functools.partial(next_kernel, b),
+        kernel, scratch = first_kernel, [pltpu.VMEM((MEMBERS * 8, LANES), F32)]
+        operands = (near, listed, weight, observed, noise)
+        in_specs = [
+            pl.BlockSpec((MEMBERS, 16, LANES), lambda i: (0, BULK // 16, 0))
+        ] + list_blocks(b, 4)
+    else:
+        kernel, scratch = next_kernel, []
+        operands = (near, far, side, weight, observed, noise, own, total)
+        in_specs = (
+            [whole(LANES, LANES)] * 2
+            + list_blocks(b, 4)
+            + [whole(*own.shape), whole(LANES, LANES)]
+        )
+    sent, total, *own = pl.pallas_call(
+        kernel,
         grid=(1,),
-        in_specs=[whole(LANES, LANES)] * 2
-        + [square] * 4
-        + [whole(SLOTS, LANES), whole(LANES, LANES)],
-        out_specs=out_specs,
+        in_specs=in_specs,
+        out_specs=[whole(*s.shape) for s in out_shape],
         out_shape=out_shape,
+        scratch_shapes=scratch,
         compiler_params=params,
         cost_estimate=cost,
-    )(near, far, side, weight, observed, noise, own, total)
+    )(*operands)
+    return sent, own[0] if own else None, total
 
 
 def select_kernel(b, slot_ref, rows_ref, out_ref, wide_ref, found_ref):
@@ -399,40 +402,52 @@
 
 ROWS = 32
 CHUNKS = BULK // ROWS
-
-
-def apply_kernel(total_ref, x_ref, out_ref, in_ref, end_ref, new_ref, flat_ref, in_sems, out_sems):
+LOADS = 8
+
+
+def last_kernel(near_ref, far_ref, side_ref, weight_ref, observed_ref, noise_ref, total_ref, x_ref,
+                out_ref, in_ref, new_ref, flat_ref, in_sems, out_sems):
+    share = MEMBERS // LOADS
     loads = [
-        pltpu.make_async_copy(x_ref.at[:, pl.ds(i * ROWS, ROWS), :], in_ref.at[i], in_sems.at[i])
-        for i in range(CHUNKS)
+        pltpu.make_async_copy(
+            x_ref.at[pl.ds(i * share, share)], in_ref.at[pl.ds(i * share, share)], in_sems.at[i]
+        )
+        for i in range(LOADS)
     ]
-    loads.append(
-        pltpu.make_async_copy(x_ref.at[:, pl.ds(BULK, 8), :], end_ref, in_sems.at[CHUNKS])
-    )
     for load in loads:
         load.start()
-    total = total_ref[...]
-    rows_ref = flat_ref.reshape(MEMBERS * (ROWS + 8), LANES)
-
-    def row(v):
+    prior = prior_of(side_ref, near_ref, far_ref)
+    transform = transform_of(prior, weight_ref[0], observed_ref[0], noise_ref[0])
+    exact = dot(total_ref[...], transform, HIGHEST).T
+    high = exact.astype(BF16)
+    total = jnp.concatenate([high, (exact - high.astype(F32)).astype(BF16)], axis=1)
+
+    def spread(i, part, parts):
+        held = min(ROWS, SENT - i * ROWS)
+        members = slice(part * MEMBERS // parts, (part + 1) * MEMBERS // parts)
+        rows = in_ref[members, i * ROWS : i * ROWS + held, :]
+        flat_ref[i % 2, members, 0:held, :] = rows.astype(F32)
+
+    def row(i, v):
+        rows_ref = flat_ref.at[i % 2].reshape(MEMBERS * (ROWS + 8), LANES)
         return rows_ref[pl.ds(v, MEMBERS, stride=ROWS + 8), :].astype(BF16)
 
     def transformed(x):
         return dot(total, jnp.concatenate([x, x], axis=0)).astype(BF16)
 
+    for part, load in enumerate(loads):
+        load.wait()
+        spread(0, part, LOADS)
     stores = []
     for i in range(CHUNKS + 1):
-        loads[i].wait()
-        number = ROWS if i < CHUNKS else REST
-        if i < CHUNKS:
-            flat_ref[:, 0:ROWS, :] = in_ref[i].astype(F32)
-        else:
-            flat_ref[:, 0:8, :] = end_ref[...].astype(F32)
+        first, number = i * ROWS, (ROWS if i < CHUNKS else REST)
         for v in range(0, number, 2):
-            y = transformed(jnp.concatenate([row(v), row(v + 1)], axis=1))
+            if i < CHUNKS:
+                spread(i + 1, v // 2, ROWS // 2)
+            y = transformed(jnp.concatenate([row(i, v), row(i, v + 1)], axis=1))
             for k in range(min(2, number - v)):
-                new_ref[i * ROWS + v + k] = y[:, k * LANES : (k + 1) * LANES]
-        places = pl.ds(i * ROWS, number)
+                new_ref[first + v + k] = y[:, k * LANES : (k + 1) * LANES]
+        places = pl.ds(first, number)
         stores.append(
             pltpu.make_async_copy(new_ref.at[places], out_ref.at[places], out_sems.at[i])
         )
@@ -441,25 +456,26 @@
         store.wait()
 
 
-def apply(total, x):
+def finish(near, far, lists_of, total, x):
+    b = BATCHES - 1
+    weight, observed, noise, _, side = lists_of[:5]
     return pl.pallas_call(
-        apply_kernel,
-        in_specs=[
-            pl.BlockSpec(memory_space=pltpu.VMEM),
-            pl.BlockSpec(memory_space=pl.ANY),
-        ],
+        last_kernel,
+        grid=(1,),
+        in_specs=[whole(LANES, LANES)] * 2
+        + list_blocks(b, 4)
+        + [whole(LANES, LANES), pl.BlockSpec(memory_space=pl.ANY)],
         out_specs=pl.BlockSpec(memory_space=pl.ANY),
         out_shape=jax.ShapeDtypeStruct((FIELDS, MEMBERS, LANES), BF16),
         scratch_shapes=[
-            pltpu.VMEM((CHUNKS, MEMBERS, ROWS, LANES), BF16),
-            pltpu.VMEM((MEMBERS, 8, LANES), BF16),
+            pltpu.VMEM((MEMBERS, SENT, LANES), BF16),
             pltpu.VMEM((FIELDS, MEMBERS, LANES), BF16),
-            pltpu.VMEM((MEMBERS, ROWS + 8, LANES), F32),
-            pltpu.SemaphoreType.DMA((CHUNKS + 1,)),
+            pltpu.VMEM((2, MEMBERS, ROWS + 8, LANES), F32),
+            pltpu.SemaphoreType.DMA((LOADS,)),
             pltpu.SemaphoreType.DMA((CHUNKS + 1,)),
         ],
-        compiler_params=pltpu.CompilerParams(vmem_limit_bytes=60_000_000),
-    )(total, x)
+        compiler_params=pltpu.CompilerParams(vmem_limit_bytes=24 * 1024 * 1024),
+    )(near, far, side, weight, observed, noise, total, x)
 
 
 def exchange(x, groups=None):
@@ -501,11 +517,9 @@
         rows = to_chips(sent).reshape(PAIRS * OWN_MAX, LANES)
         far = swap(select(b, slots_there, rows))
         near = select(b, slots, rows)
-        if b == BATCHES - 1:
-            (total,) = solve(b, near, far, lists_of, own, total)
-        else:
+        if b < BATCHES - 1:
             sent, own, total = solve(b, near, far, lists_of, own, total)
-    return apply(total, fields).transpose(1, 0, 2)
+    return finish(near, far, lists_of, total, fields).transpose(1, 0, 2)
 
 
 def solution(mesh):

time: 189 us -> 187 us (0.989)
  Pallas kernels: 32.5 us -> 30.6 us
    pallas_call x5 -> x4, Pallas kernels: 19.1 us -> 17.2 us  [the longest x1 8.8 us: finish(): pl.pallas_call(last_kernel, grid=(1,), in_specs=[whole(LANES, LANES)] * 2...]
where the time goes in v4:
time: 187 us; the launch traced here: 186 us
  waiting for transfers between devices  89.6 us (48%)
  blocking collectives  46.1 us (25%)
  Pallas kernels  30.6 us (16%)
  starting transfers between devices  19.7 us (11%)
    all_to_all x1, waiting for transfers between devices, exchange(): lax.all_to_all(x, AXES, split_axis=0, concat_axis=0, axis_index_groups=gr...  88.3 us
    all_to_all x3, blocking collectives, exchange(): lax.all_to_all(x, AXES, split_axis=0, concat_axis=0, axis_index_groups=gr...  46.1 us
    all_to_all x1, starting transfers between devices, exchange(): lax.all_to_all(x, AXES, split_axis=0, concat_axis=0, axis_index_groups=gr...  11.9 us
    pallas_call x1, Pallas kernels, finish(): pl.pallas_call(last_kernel, grid=(1,), in_specs=[whole(LANES, LANES)] * 2...  8.8 us
    pallas_call x3, Pallas kernels, solve(): pl.pallas_call(kernel, grid=(1,), in_specs=in_specs, out_specs=[whole(*s....  8.38 us
    ppermute x4, starting transfers between devices, swap(): return lax.ppermute(x, 'tile', [(i, i ^ 1) for i in range(size)])  7.81 us
    pallas_call x1, Pallas kernels, pick(): pl.pallas_call(pick_kernel, in_specs=[pl.BlockSpec(memory_space=pl.ANY),...  7.52 us
    pallas_call x6, Pallas kernels, select(): pl.pallas_call(functools.partial(select_kernel, b), grid=(1,), in_specs=[...  4.19 us
  transfers between devices with their start and end apart: 5, of which 5 were waited for; matrix products, arithmetic and copies ran while one was open for 0% of the time, Pallas kernels for 2%

profile of v4, /device:TPU:1, one launch (start us, length us, event | category | flops | bytes accessed | tf_op | source)
XLA Modules:
  0.0 186.3 jit_solution(8882551905080692385)
XLA Ops:
  0.0 7.5 %shard_map.91 = bf16[128,232,128]{2,1,0:T(8,128)(2,1)} custom-call(bf16[1,227,16384]{2,1,0:T(8,128)(2,1)} %x_ref.1, s32[4,1,512]{2,1,0:T(1,128)} %bitcast.11, s32[4,512]{1,0:T(4,128)} %field_ref.1, s32[4,512]{1,0:T(4,128)} %stack_ref.1), custom_call_target="tpu_custom_call" | custom-call | tf_op jit(solution)/shard_map/pallas_call | solution.py:164
  7.5 0.0 copy-start.3
  7.5 0.0 copy-start
  7.6 0.0 copy-start.1
  7.6 0.0 copy-start.2
  7.6 0.0 copy-start.4
  7.6 0.0 copy-start.5
  7.6 11.9 %all-to-all-start = ((bf16[128,232,128]{2,1,0:T(8,128)(2,1)}), bf16[128,232,128]{2,1,0:T(8,128)(2,1)}, u32[]{:S(2)}, u32[]{:S(2)}) async-start(bf16[128,232,128]{2,1,0:T(8,128)(2,1)} %shard_map.91), calls=%async_computation | async-start | bytes 15204352 | tf_op jit(solution)/shard_map/all_to_all | solution.py:482
  19.5 1.2 collective-permute-start
  20.7 0.8 collective-permute-done.there_ref
  21.6 0.0 copy-done.2
  21.6 1.7 shard_map.92
  23.2 88.3 %all-to-all-done.message_ref.x_ref = bf16[128,232,128]{2,1,0:T(8,128)(2,1)} async-done(((bf16[128,232,128]{2,1,0:T(8,128)(2,1)}), bf16[128,232,128]{2,1,0:T(8,128)(2,1)}, u32[]{:S(2)}, u32[]{:S(2)}) %all-to-all-start) | async-done | bytes 7602208 | tf_op jit(solution)/shard_map/all_to_all | solution.py:482
  111.6 3.7 %shard_map.93 = (s16[64,16,128]{2,1,0:T(8,128)(2,1)S(1)}, f32[128,128]{1,0:T(8,128)S(1)}, f32[32,128]{1,0:T(8,128)S(1)}) custom-call(bf16[128,232,128]{2,1,0:T(8,128)(2,1)} %all-to-all-done.message_ref.x_ref, s32[4,128,128]{2,1,0:T(8,128)S(1)} %get-tuple-element.41.listed_ref, f32[4,128,128]{2,1,0:T(8,128)S(1)} %get-tuple-element.42.weight_ref, ...), custom_call_target="tpu_custom_call" | custom-call | flops 400000000 | bytes 4000000 | tf_op jit(solution)/shard_map/pallas_call | solution.py:367
  115.3 18.5 %all_to_all.20 = s16[64,16,128]{2,1,0:T(8,128)(2,1)S(1)} all-to-all(s16[64,16,128]{2,1,0:T(8,128)(2,1)S(1)} %get-tuple-element.45), channel_id=1, replica_groups={{0,2,4,6,8,10,12,14,16,18,20,22,24,26,28,30,32,34,36,38,40,42,44,46,48,..., dimensions={0} | all-to-all | bytes 524288 | tf_op jit(solution)/shard_map/all_to_all | solution.py:482
  133.8 0.7 shard_map.95
  134.5 2.2 %collective-permute-start.1 = (s16[128,128]{1,0:T(8,128)(2,1)S(1)}, s16[128,128]{1,0:T(8,128)(2,1)S(1)}, u32[]{:S(2)}, u32[]{:S(2)}) collective-permute-start(s16[128,128]{1,0:T(8,128)(2,1)S(1)} %shard_map.95), channel_id=1, source_target_pairs={{0,1},{1,0},{2,3},{3,2},{4,5},{5,4},{6,7},{7,6},{8,9},{9,8},{10,11... | collective-permute-start | bytes 98312 | tf_op jit(solution)/shard_map/ppermute | solution.py:491
  136.6 0.7 shard_map.94.near_ref
  137.3 0.2 collective-permute-done.1.far_ref
  137.5 2.3 %shard_map.96 = (s16[64,16,128]{2,1,0:T(8,128)(2,1)S(1)}, f32[128,128]{1,0:T(8,128)S(1)}, f32[16,128]{1,0:T(8,128)S(1)}) custom-call(s16[128,128]{1,0:T(8,128)(2,1)S(1)} %shard_map.94.near_ref, s16[128,128]{1,0:T(8,128)(2,1)S(1)} %collective-permute-done.1.far_ref, f32[4,128,128]{2,1,0:T(8,128)S(1)} %get-tuple-element.47.side_ref, ...), custom_call_target="tpu_custom_call" | custom-call | flops 400000000 | bytes 4000000 | tf_op jit(solution)/shard_map/pallas_call | solution.py:367
  139.9 13.8 %all_to_all.21 = s16[64,16,128]{2,1,0:T(8,128)(2,1)S(1)} all-to-all(s16[64,16,128]{2,1,0:T(8,128)(2,1)S(1)} %get-tuple-element.50), channel_id=1, replica_groups={{0,2,4,6,8,10,12,14,16,18,20,22,24,26,28,30,32,34,36,38,40,42,44,46,48,..., dimensions={0} | all-to-all | bytes 524288 | tf_op jit(solution)/shard_map/all_to_all | solution.py:482
  153.6 0.7 shard_map.98
  154.3 2.3 %collective-permute-start.2 = (s16[128,128]{1,0:T(8,128)(2,1)S(1)}, s16[128,128]{1,0:T(8,128)(2,1)S(1)}, u32[]{:S(2)}, u32[]{:S(2)}) collective-permute-start(s16[128,128]{1,0:T(8,128)(2,1)S(1)} %shard_map.98), channel_id=1, source_target_pairs={{0,1},{1,0},{2,3},{3,2},{4,5},{5,4},{6,7},{7,6},{8,9},{9,8},{10,11... | collective-permute-start | bytes 98312 | tf_op jit(solution)/shard_map/ppermute | solution.py:491
  156.6 0.7 shard_map.97.near_ref
  157.3 0.2 collective-permute-done.2.far_ref
  157.5 2.3 %shard_map.99 = (s16[64,16,128]{2,1,0:T(8,128)(2,1)S(1)}, f32[128,128]{1,0:T(8,128)S(1)}) custom-call(s16[128,128]{1,0:T(8,128)(2,1)S(1)} %shard_map.97.near_ref, s16[128,128]{1,0:T(8,128)(2,1)S(1)} %collective-permute-done.2.far_ref, f32[4,128,128]{2,1,0:T(8,128)S(1)} %get-tuple-element.47.side_ref, f32[4,128,128]{2,1,0:T(8,128)S(1)} %get-tuple-element.42.weight_ref, ...), custom_call_target="tpu_custom_call" | custom-call | flops 400000000 | bytes 4000000 | tf_op jit(solution)/shard_map/pallas_call | solution.py:367
  159.8 13.8 %all_to_all.22 = s16[64,16,128]{2,1,0:T(8,128)(2,1)S(1)} all-to-all(s16[64,16,128]{2,1,0:T(8,128)(2,1)S(1)} %get-tuple-element.53), channel_id=1, replica_groups={{0,2,4,6,8,10,12,14,16,18,20,22,24,26,28,30,32,34,36,38,40,42,44,46,48,..., dimensions={0} | all-to-all | bytes 524288 | tf_op jit(solution)/shard_map/all_to_all | solution.py:482
  173.6 0.7 shard_map.101
  174.3 2.1 %collective-permute-start.3 = (s16[128,128]{1,0:T(8,128)(2,1)S(1)}, s16[128,128]{1,0:T(8,128)(2,1)S(1)}, u32[]{:S(2)}, u32[]{:S(2)}) collective-permute-start(s16[128,128]{1,0:T(8,128)(2,1)S(1)} %shard_map.101), channel_id=1, source_target_pairs={{0,1},{1,0},{2,3},{3,2},{4,5},{5,4},{6,7},{7,6},{8,9},{9,8},{10,11... | collective-permute-start | bytes 98312 | tf_op jit(solution)/shard_map/ppermute | solution.py:491
  176.4 0.7 shard_map.100.near_ref
  177.1 0.2 collective-permute-done.3.far_ref
  177.3 8.8 %shard_map.102 = bf16[227,128,128]{2,1,0:T(8,128)(2,1)} custom-call(s16[128,128]{1,0:T(8,128)(2,1)S(1)} %shard_map.100.near_ref, s16[128,128]{1,0:T(8,128)(2,1)S(1)} %collective-permute-done.3.far_ref, f32[4,128,128]{2,1,0:T(8,128)S(1)} %get-tuple-element.47.side_ref, f32[4,128,128]{2,1,0:T(8,128)S(1)} %get-tuple-element.42.weight_ref, ...), custom_call_target="tpu_custom_call" | custom-call | tf_op jit(solution)/shard_map/pallas_call | solution.py:462
  (5 shorter events, 0.0 us)
Async XLA Ops:
  7.5 12.0 %copy-start.3 = (s32[4,1,128]{2,1,0:T(1,128)S(1)}, s32[4,1,128]{2,1,0:T(1,128)}, u32[]{:S(2)}) copy-start(s32[4,1,128]{2,1,0:T(1,128)} %roster_ref.1) | copy-start | bytes 6148
  7.5 14.0 %copy-start = (s32[4,512,1]{1,2,0:T(1,128)S(1)}, s32[4,512,1]{1,2,0:T(1,128)}, u32[]{:S(2)}) copy-start(s32[4,512,1]{1,2,0:T(1,128)} %param.13) | copy-start | bytes 24580
  7.6 14.0 %copy-start.1 = (f32[4,512]{1,0:T(4,128)S(1)}, f32[4,512]{1,0:T(4,128)}, u32[]{:S(2)}) copy-start(f32[4,512]{1,0:T(4,128)} %reading_ref.1) | copy-start | bytes 24580
  7.6 14.0 %copy-start.2 = (f32[4,512]{1,0:T(4,128)S(1)}, f32[4,512]{1,0:T(4,128)}, u32[]{:S(2)}) copy-start(f32[4,512]{1,0:T(4,128)} %variance_ref.1) | copy-start | bytes 24580
  7.6 14.0 %copy-start.4 = (s32[4,1,128]{2,1,0:T(1,128)S(1)}, s32[4,1,128]{2,1,0:T(1,128)}, u32[]{:S(2)}) copy-start(s32[4,1,128]{2,1,0:T(1,128)} %kind_ref.1) | copy-start | bytes 6148
  7.6 14.0 %copy-start.5 = (s32[4]{0:T(128)S(1)}, s32[4]{0:T(128)}, u32[]{:S(2)}) copy-start(s32[4]{0:T(128)} %used_ref) | copy-start | bytes 52
  7.6 104.0 %all-to-all-start = ((bf16[128,232,128]{2,1,0:T(8,128)(2,1)}), bf16[128,232,128]{2,1,0:T(8,128)(2,1)}, u32[]{:S(2)}, u32[]{:S(2)}) async-start(bf16[128,232,128]{2,1,0:T(8,128)(2,1)} %shard_map.91), calls=%async_computation | async-start | bytes 15204352 | tf_op jit(solution)/shard_map/all_to_all | solution.py:482
  19.5 2.0 %collective-permute-start = (s32[4,1,128]{2,1,0:T(1,128)S(1)}, s32[4,1,128]{2,1,0:T(1,128)S(1)}, u32[]{:S(2)}, u32[]{:S(2)}) collective-permute-start(s32[4,1,128]{2,1,0:T(1,128)S(1)} %copy-done.3), channel_id=1, source_target_pairs={{0,1},{1,0},{2,3},{3,2},{4,5},{5,4},{6,7},{7,6},{8,9},{9,8},{10,11... | collective-permute-start | bytes 6152 | tf_op jit(solution)/shard_map/ppermute | solution.py:491
  134.5 3.0 %collective-permute-start.1 = (s16[128,128]{1,0:T(8,128)(2,1)S(1)}, s16[128,128]{1,0:T(8,128)(2,1)S(1)}, u32[]{:S(2)}, u32[]{:S(2)}) collective-permute-start(s16[128,128]{1,0:T(8,128)(2,1)S(1)} %shard_map.95), channel_id=1, source_target_pairs={{0,1},{1,0},{2,3},{3,2},{4,5},{5,4},{6,7},{7,6},{8,9},{9,8},{10,11... | collective-permute-start | bytes 98312 | tf_op jit(solution)/shard_map/ppermute | solution.py:491
  154.3 3.2 %collective-permute-start.2 = (s16[128,128]{1,0:T(8,128)(2,1)S(1)}, s16[128,128]{1,0:T(8,128)(2,1)S(1)}, u32[]{:S(2)}, u32[]{:S(2)}) collective-permute-start(s16[128,128]{1,0:T(8,128)(2,1)S(1)} %shard_map.98), channel_id=1, source_target_pairs={{0,1},{1,0},{2,3},{3,2},{4,5},{5,4},{6,7},{7,6},{8,9},{9,8},{10,11... | collective-permute-start | bytes 98312 | tf_op jit(solution)/shard_map/ppermute | solution.py:491
  174.3 3.0 %collective-permute-start.3 = (s16[128,128]{1,0:T(8,128)(2,1)S(1)}, s16[128,128]{1,0:T(8,128)(2,1)S(1)}, u32[]{:S(2)}, u32[]{:S(2)}) collective-permute-start(s16[128,128]{1,0:T(8,128)(2,1)S(1)} %shard_map.101), channel_id=1, source_target_pairs={{0,1},{1,0},{2,3},{3,2},{4,5},{5,4},{6,7},{7,6},{8,9},{9,8},{10,11... | collective-permute-start | bytes 98312 | tf_op jit(solution)/shard_map/ppermute | solution.py:491

commit v5 on v4

--- a/solution.py
+++ b/solution.py
@@ -400,51 +400,31 @@
     )(slots, rows)
 
 
-ROWS = 32
+ROWS = 112
 CHUNKS = BULK // ROWS
-LOADS = 8
 
 
 def last_kernel(near_ref, far_ref, side_ref, weight_ref, observed_ref, noise_ref, total_ref, x_ref,
-                out_ref, in_ref, new_ref, flat_ref, in_sems, out_sems):
-    share = MEMBERS // LOADS
-    loads = [
-        pltpu.make_async_copy(
-            x_ref.at[pl.ds(i * share, share)], in_ref.at[pl.ds(i * share, share)], in_sems.at[i]
-        )
-        for i in range(LOADS)
-    ]
-    for load in loads:
-        load.start()
+                out_ref, in_ref, new_ref, in_sem, out_sems):
+    load = pltpu.make_async_copy(x_ref, in_ref, in_sem)
+    load.start()
     prior = prior_of(side_ref, near_ref, far_ref)
     transform = transform_of(prior, weight_ref[0], observed_ref[0], noise_ref[0])
     exact = dot(total_ref[...], transform, HIGHEST).T
     high = exact.astype(BF16)
     total = jnp.concatenate([high, (exact - high.astype(F32)).astype(BF16)], axis=1)
 
-    def spread(i, part, parts):
-        held = min(ROWS, SENT - i * ROWS)
-        members = slice(part * MEMBERS // parts, (part + 1) * MEMBERS // parts)
-        rows = in_ref[members, i * ROWS : i * ROWS + held, :]
-        flat_ref[i % 2, members, 0:held, :] = rows.astype(F32)
-
-    def row(i, v):
-        rows_ref = flat_ref.at[i % 2].reshape(MEMBERS * (ROWS + 8), LANES)
-        return rows_ref[pl.ds(v, MEMBERS, stride=ROWS + 8), :].astype(BF16)
-
     def transformed(x):
         return dot(total, jnp.concatenate([x, x], axis=0)).astype(BF16)
 
-    for part, load in enumerate(loads):
-        load.wait()
-        spread(0, part, LOADS)
+    load.wait()
     stores = []
     for i in range(CHUNKS + 1):
         first, number = i * ROWS, (ROWS if i < CHUNKS else REST)
         for v in range(0, number, 2):
-            if i < CHUNKS:
-                spread(i + 1, v // 2, ROWS // 2)
-            y = transformed(jnp.concatenate([row(i, v), row(i, v + 1)], axis=1))
+            if v % 8 == 0:
+                turned = jnp.swapaxes(in_ref[:, first + v : first + v + 8, :], 0, 1)
+            y = transformed(jnp.concatenate([turned[v % 8], turned[v % 8 + 1]], axis=1))
             for k in range(min(2, number - v)):
                 new_ref[first + v + k] = y[:, k * LANES : (k + 1) * LANES]
         places = pl.ds(first, number)
@@ -470,8 +450,7 @@
         scratch_shapes=[
             pltpu.VMEM((MEMBERS, SENT, LANES), BF16),
             pltpu.VMEM((FIELDS, MEMBERS, LANES), BF16),
-            pltpu.VMEM((2, MEMBERS, ROWS + 8, LANES), F32),
-            pltpu.SemaphoreType.DMA((LOADS,)),
+            pltpu.SemaphoreType.DMA,
             pltpu.SemaphoreType.DMA((CHUNKS + 1,)),
         ],
         compiler_params=pltpu.CompilerParams(vmem_limit_bytes=24 * 1024 * 1024),

time: 187 us -> 187 us (level)
  no operation moved by 1% of the time
where the time goes in v5:
time: 187 us; the launch traced here: 186 us
  waiting for transfers between devices  89.6 us (48%)
  blocking collectives  46.9 us (25%)
  Pallas kernels  30.6 us (16%)
  starting transfers between devices  18.9 us (10%)
    all_to_all x1, waiting for transfers between devices, exchange(): lax.all_to_all(x, AXES, split_axis=0, concat_axis=0, axis_index_groups=gr...  88.3 us
    all_to_all x3, blocking collectives, exchange(): lax.all_to_all(x, AXES, split_axis=0, concat_axis=0, axis_index_groups=gr...  46.9 us
    all_to_all x1, starting transfers between devices, exchange(): lax.all_to_all(x, AXES, split_axis=0, concat_axis=0, axis_index_groups=gr...  11.9 us
    pallas_call x1, Pallas kernels, finish(): pl.pallas_call(last_kernel, grid=(1,), in_specs=[whole(LANES, LANES)] * 2...  8.65 us
    pallas_call x3, Pallas kernels, solve(): pl.pallas_call(kernel, grid=(1,), in_specs=in_specs, out_specs=[whole(*s....  8.59 us
    pallas_call x1, Pallas kernels, pick(): pl.pallas_call(pick_kernel, in_specs=[pl.BlockSpec(memory_space=pl.ANY),...  7.52 us
    ppermute x4, starting transfers between devices, swap(): return lax.ppermute(x, 'tile', [(i, i ^ 1) for i in range(size)])  7 us
    pallas_call x6, Pallas kernels, select(): pl.pallas_call(functools.partial(select_kernel, b), grid=(1,), in_specs=[...  4.19 us
  transfers between devices with their start and end apart: 5, of which 5 were waited for; matrix products, arithmetic and copies ran while one was open for 0% of the time, Pallas kernels for 2%

profile of v5, /device:TPU:1, one launch (start us, length us, event | category | flops | bytes accessed | tf_op | source)
XLA Modules:
  0.0 186.3 jit_solution(12957536313627686071)
XLA Ops:
  0.0 7.5 %shard_map.91 = bf16[128,232,128]{2,1,0:T(8,128)(2,1)} custom-call(bf16[1,227,16384]{2,1,0:T(8,128)(2,1)} %x_ref.1, s32[4,1,512]{2,1,0:T(1,128)} %bitcast.11, s32[4,512]{1,0:T(4,128)} %field_ref.1, s32[4,512]{1,0:T(4,128)} %stack_ref.1), custom_call_target="tpu_custom_call" | custom-call | tf_op jit(solution)/shard_map/pallas_call | solution.py:164
  7.5 0.0 copy-start.3
  7.5 0.0 copy-start
  7.6 0.0 copy-start.1
  7.6 0.0 copy-start.2
  7.6 0.0 copy-start.4
  7.6 0.0 copy-start.5
  7.6 11.9 %all-to-all-start = ((bf16[128,232,128]{2,1,0:T(8,128)(2,1)}), bf16[128,232,128]{2,1,0:T(8,128)(2,1)}, u32[]{:S(2)}, u32[]{:S(2)}) async-start(bf16[128,232,128]{2,1,0:T(8,128)(2,1)} %shard_map.91), calls=%async_computation | async-start | bytes 15204352 | tf_op jit(solution)/shard_map/all_to_all | solution.py:461
  19.5 1.2 collective-permute-start
  20.7 0.8 collective-permute-done.there_ref
  21.6 0.0 copy-done.2
  21.6 1.7 shard_map.92
  23.2 88.3 %all-to-all-done.message_ref.x_ref = bf16[128,232,128]{2,1,0:T(8,128)(2,1)} async-done(((bf16[128,232,128]{2,1,0:T(8,128)(2,1)}), bf16[128,232,128]{2,1,0:T(8,128)(2,1)}, u32[]{:S(2)}, u32[]{:S(2)}) %all-to-all-start) | async-done | bytes 7602208 | tf_op jit(solution)/shard_map/all_to_all | solution.py:461
  111.6 3.7 %shard_map.93 = (s16[64,16,128]{2,1,0:T(8,128)(2,1)S(1)}, f32[128,128]{1,0:T(8,128)S(1)}, f32[32,128]{1,0:T(8,128)S(1)}) custom-call(bf16[128,232,128]{2,1,0:T(8,128)(2,1)} %all-to-all-done.message_ref.x_ref, s32[4,128,128]{2,1,0:T(8,128)S(1)} %get-tuple-element.41.listed_ref, f32[4,128,128]{2,1,0:T(8,128)S(1)} %get-tuple-element.42.weight_ref, ...), custom_call_target="tpu_custom_call" | custom-call | flops 400000000 | bytes 4000000 | tf_op jit(solution)/shard_map/pallas_call | solution.py:367
  115.3 18.5 %all_to_all.20 = s16[64,16,128]{2,1,0:T(8,128)(2,1)S(1)} all-to-all(s16[64,16,128]{2,1,0:T(8,128)(2,1)S(1)} %get-tuple-element.45), channel_id=1, replica_groups={{0,2,4,6,8,10,12,14,16,18,20,22,24,26,28,30,32,34,36,38,40,42,44,46,48,..., dimensions={0} | all-to-all | bytes 524288 | tf_op jit(solution)/shard_map/all_to_all | solution.py:461
  133.8 0.7 shard_map.95
  134.5 2.2 %collective-permute-start.1 = (s16[128,128]{1,0:T(8,128)(2,1)S(1)}, s16[128,128]{1,0:T(8,128)(2,1)S(1)}, u32[]{:S(2)}, u32[]{:S(2)}) collective-permute-start(s16[128,128]{1,0:T(8,128)(2,1)S(1)} %shard_map.95), channel_id=1, source_target_pairs={{0,1},{1,0},{2,3},{3,2},{4,5},{5,4},{6,7},{7,6},{8,9},{9,8},{10,11... | collective-permute-start | bytes 98312 | tf_op jit(solution)/shard_map/ppermute | solution.py:470
  136.6 0.7 shard_map.94.near_ref
  137.3 0.2 collective-permute-done.1.far_ref
  137.5 2.5 %shard_map.96 = (s16[64,16,128]{2,1,0:T(8,128)(2,1)S(1)}, f32[128,128]{1,0:T(8,128)S(1)}, f32[16,128]{1,0:T(8,128)S(1)}) custom-call(s16[128,128]{1,0:T(8,128)(2,1)S(1)} %shard_map.94.near_ref, s16[128,128]{1,0:T(8,128)(2,1)S(1)} %collective-permute-done.1.far_ref, f32[4,128,128]{2,1,0:T(8,128)S(1)} %get-tuple-element.47.side_ref, ...), custom_call_target="tpu_custom_call" | custom-call | flops 400000000 | bytes 4000000 | tf_op jit(solution)/shard_map/pallas_call | solution.py:367
  140.1 14.2 %all_to_all.21 = s16[64,16,128]{2,1,0:T(8,128)(2,1)S(1)} all-to-all(s16[64,16,128]{2,1,0:T(8,128)(2,1)S(1)} %get-tuple-element.50), channel_id=1, replica_groups={{0,2,4,6,8,10,12,14,16,18,20,22,24,26,28,30,32,34,36,38,40,42,44,46,48,..., dimensions={0} | all-to-all | bytes 524288 | tf_op jit(solution)/shard_map/all_to_all | solution.py:461
  154.2 0.7 shard_map.98
  154.9 1.9 %collective-permute-start.2 = (s16[128,128]{1,0:T(8,128)(2,1)S(1)}, s16[128,128]{1,0:T(8,128)(2,1)S(1)}, u32[]{:S(2)}, u32[]{:S(2)}) collective-permute-start(s16[128,128]{1,0:T(8,128)(2,1)S(1)} %shard_map.98), channel_id=1, source_target_pairs={{0,1},{1,0},{2,3},{3,2},{4,5},{5,4},{6,7},{7,6},{8,9},{9,8},{10,11... | collective-permute-start | bytes 98312 | tf_op jit(solution)/shard_map/ppermute | solution.py:470
  156.8 0.7 shard_map.97.near_ref
  157.5 0.2 collective-permute-done.2.far_ref
  157.7 2.3 %shard_map.99 = (s16[64,16,128]{2,1,0:T(8,128)(2,1)S(1)}, f32[128,128]{1,0:T(8,128)S(1)}) custom-call(s16[128,128]{1,0:T(8,128)(2,1)S(1)} %shard_map.97.near_ref, s16[128,128]{1,0:T(8,128)(2,1)S(1)} %collective-permute-done.2.far_ref, f32[4,128,128]{2,1,0:T(8,128)S(1)} %get-tuple-element.47.side_ref, f32[4,128,128]{2,1,0:T(8,128)S(1)} %get-tuple-element.42.weight_ref, ...), custom_call_target="tpu_custom_call" | custom-call | flops 400000000 | bytes 4000000 | tf_op jit(solution)/shard_map/pallas_call | solution.py:367
  160.0 14.2 %all_to_all.22 = s16[64,16,128]{2,1,0:T(8,128)(2,1)S(1)} all-to-all(s16[64,16,128]{2,1,0:T(8,128)(2,1)S(1)} %get-tuple-element.53), channel_id=1, replica_groups={{0,2,4,6,8,10,12,14,16,18,20,22,24,26,28,30,32,34,36,38,40,42,44,46,48,..., dimensions={0} | all-to-all | bytes 524288 | tf_op jit(solution)/shard_map/all_to_all | solution.py:461
  174.2 0.7 shard_map.101
  174.9 1.7 collective-permute-start.3
  176.6 0.7 shard_map.100.near_ref
  177.3 0.2 collective-permute-done.3.far_ref
  177.5 8.7 %shard_map.102 = bf16[227,128,128]{2,1,0:T(8,128)(2,1)} custom-call(s16[128,128]{1,0:T(8,128)(2,1)S(1)} %shard_map.100.near_ref, s16[128,128]{1,0:T(8,128)(2,1)S(1)} %collective-permute-done.3.far_ref, f32[4,128,128]{2,1,0:T(8,128)S(1)} %get-tuple-element.47.side_ref, f32[4,128,128]{2,1,0:T(8,128)S(1)} %get-tuple-element.42.weight_ref, ...), custom_call_target="tpu_custom_call" | custom-call | tf_op jit(solution)/shard_map/pallas_call | solution.py:442
  (5 shorter events, 0.0 us)
Async XLA Ops:
  7.5 12.0 %copy-start.3 = (s32[4,1,128]{2,1,0:T(1,128)S(1)}, s32[4,1,128]{2,1,0:T(1,128)}, u32[]{:S(2)}) copy-start(s32[4,1,128]{2,1,0:T(1,128)} %roster_ref.1) | copy-start | bytes 6148
  7.5 14.0 %copy-start = (s32[4,512,1]{1,2,0:T(1,128)S(1)}, s32[4,512,1]{1,2,0:T(1,128)}, u32[]{:S(2)}) copy-start(s32[4,512,1]{1,2,0:T(1,128)} %param.13) | copy-start | bytes 24580
  7.6 14.0 %copy-start.1 = (f32[4,512]{1,0:T(4,128)S(1)}, f32[4,512]{1,0:T(4,128)}, u32[]{:S(2)}) copy-start(f32[4,512]{1,0:T(4,128)} %reading_ref.1) | copy-start | bytes 24580
  7.6 14.0 %copy-start.2 = (f32[4,512]{1,0:T(4,128)S(1)}, f32[4,512]{1,0:T(4,128)}, u32[]{:S(2)}) copy-start(f32[4,512]{1,0:T(4,128)} %variance_ref.1) | copy-start | bytes 24580
  7.6 14.0 %copy-start.4 = (s32[4,1,128]{2,1,0:T(1,128)S(1)}, s32[4,1,128]{2,1,0:T(1,128)}, u32[]{:S(2)}) copy-start(s32[4,1,128]{2,1,0:T(1,128)} %kind_ref.1) | copy-start | bytes 6148
  7.6 14.0 %copy-start.5 = (s32[4]{0:T(128)S(1)}, s32[4]{0:T(128)}, u32[]{:S(2)}) copy-start(s32[4]{0:T(128)} %used_ref) | copy-start | bytes 52
  7.6 104.0 %all-to-all-start = ((bf16[128,232,128]{2,1,0:T(8,128)(2,1)}), bf16[128,232,128]{2,1,0:T(8,128)(2,1)}, u32[]{:S(2)}, u32[]{:S(2)}) async-start(bf16[128,232,128]{2,1,0:T(8,128)(2,1)} %shard_map.91), calls=%async_computation | async-start | bytes 15204352 | tf_op jit(solution)/shard_map/all_to_all | solution.py:461
  19.5 2.0 %collective-permute-start = (s32[4,1,128]{2,1,0:T(1,128)S(1)}, s32[4,1,128]{2,1,0:T(1,128)S(1)}, u32[]{:S(2)}, u32[]{:S(2)}) collective-permute-start(s32[4,1,128]{2,1,0:T(1,128)S(1)} %copy-done.3), channel_id=1, source_target_pairs={{0,1},{1,0},{2,3},{3,2},{4,5},{5,4},{6,7},{7,6},{8,9},{9,8},{10,11... | collective-permute-start | bytes 6152 | tf_op jit(solution)/shard_map/ppermute | solution.py:470
  134.5 3.0 %collective-permute-start.1 = (s16[128,128]{1,0:T(8,128)(2,1)S(1)}, s16[128,128]{1,0:T(8,128)(2,1)S(1)}, u32[]{:S(2)}, u32[]{:S(2)}) collective-permute-start(s16[128,128]{1,0:T(8,128)(2,1)S(1)} %shard_map.95), channel_id=1, source_target_pairs={{0,1},{1,0},{2,3},{3,2},{4,5},{5,4},{6,7},{7,6},{8,9},{9,8},{10,11... | collective-permute-start | bytes 98312 | tf_op jit(solution)/shard_map/ppermute | solution.py:470
  154.9 2.8 %collective-permute-start.2 = (s16[128,128]{1,0:T(8,128)(2,1)S(1)}, s16[128,128]{1,0:T(8,128)(2,1)S(1)}, u32[]{:S(2)}, u32[]{:S(2)}) collective-permute-start(s16[128,128]{1,0:T(8,128)(2,1)S(1)} %shard_map.98), channel_id=1, source_target_pairs={{0,1},{1,0},{2,3},{3,2},{4,5},{5,4},{6,7},{7,6},{8,9},{9,8},{10,11... | collective-permute-start | bytes 98312 | tf_op jit(solution)/shard_map/ppermute | solution.py:470
  174.9 2.6 %collective-permute-start.3 = (s16[128,128]{1,0:T(8,128)(2,1)S(1)}, s16[128,128]{1,0:T(8,128)(2,1)S(1)}, u32[]{:S(2)}, u32[]{:S(2)}) collective-permute-start(s16[128,128]{1,0:T(8,128)(2,1)S(1)} %shard_map.101), channel_id=1, source_target_pairs={{0,1},{1,0},{2,3},{3,2},{4,5},{5,4},{6,7},{7,6},{8,9},{9,8},{10,11... | collective-permute-start | bytes 98312 | tf_op jit(solution)/shard_map/ppermute | solution.py:470
